TPU v7x, 32 devices: a whole 2x2x4 slice. The times are simulated.
32 devices in a mesh: ctx: 16 (over z, y, x), head: 2 (over core).
Axes of the slice: x: 2, y: 2, z: 4, core: 2. Of those that a mesh axis runs over, the one named last changes fastest.
Arguments:
- softmax_query: bfloat16 [2048, 1024], P('ctx', 'head'), may hold values from -6 to 6
- softmax_key: bfloat16 [2048, 1024], P('ctx', 'head'), may hold values from -6 to 6
- softmax_value: bfloat16 [2048, 1024], P('ctx', 'head'), may hold values from -6 to 6
- document_ids: int32 [16], P('ctx'), may hold values from 0 to 3, never falling along the last dimension, each value on 1 to 12 neighbouring positions
- block_lists: int32 [16, 2], P('ctx'), may hold values from 0 to 2, all different within a row
- linear_key: bfloat16 [2048, 1024], P('ctx', 'head'), may hold values from -0.5 to 0.5
- linear_value: bfloat16 [2048, 1024], P('ctx', 'head'), may hold values from -6 to 6
- linear_decay: float32 [8, 2048], P('head', 'ctx'), may hold values from -0.7 to 0
- linear_gain: float32 [1024], P('head'), may hold values from 0.5 to 1.5
- linear_cotangent: bfloat16 [2048, 1024], P('ctx', 'head'), may hold values from -6 to 6
Outputs:
- softmax_output: bfloat16 [2048, 1024], P('ctx', 'head')
- softmax_query_grad: bfloat16 [2048, 1024], P('ctx', 'head')
- softmax_key_grad: bfloat16 [2048, 1024], P('ctx', 'head')
- softmax_value_grad: bfloat16 [2048, 1024], P('ctx', 'head')
- linear_output: bfloat16 [2048, 1024], P('ctx', 'head')
- linear_query_grad: bfloat16 [2048, 1024], P('ctx', 'head')
- linear_key_grad: bfloat16 [2048, 1024], P('ctx', 'head')
- linear_value_grad: bfloat16 [2048, 1024], P('ctx', 'head')
Inputs may be any that keep to these rules, and one draw needn't show every extreme that they name: `document_ids`: never falls from block to block; a document covers 1 to 12 blocks. `block_lists`: the entries of a row are distinct.
All inputs are finite; a program needn't handle non-finite values.
Results may differ from a plain program's by a relative error of at most 0.04.
Values may be sent and summed in bfloat16 or wider, within the bound.
A program may use at most 64 MiB of HBM per device.

v0:
```python
import math

import jax
import jax.numpy as jnp
from jax import lax
from jax.sharding import PartitionSpec as P

HD = 128
BLK = 128
WB = 4


NEG_FILL = -1e30
EPSILON = 1e-05


def passed_along(array, axis, by):
    size = lax.axis_size(axis)
    pairs = [(i, i + by) for i in range(size) if 0 <= i + by < size]
    return lax.ppermute(array, axis, pairs)


def prefix(array, axis, join, neutral, backward):
    count = lax.axis_size(axis)
    place = lax.axis_index(axis)
    ahead = count - 1 - place if backward else place
    gathered = jax.tree.map(
        lambda a, kind: lax.all_gather(a.astype(kind), axis), array, (jnp.bfloat16, jnp.bfloat16)
    )
    state = jax.tree.map(lambda a, e: jnp.zeros_like(a) + jnp.asarray(e, a.dtype), array, neutral)

    def one(lap, state):
        source = count - 1 - lap if backward else lap
        return join(
            state,
            jax.tree.map(
                lambda a, own: lax.dynamic_index_in_dim(a, source, 0, False).astype(own.dtype),
                gathered,
                array,
            ),
        )

    return lax.fori_loop(0, ahead, one, state)


def token_visible(query_blocks, lookup_segments, query_docs, key_docs, query_lists, block_total):
    offsets = query_blocks[:, None] - lookup_segments[None, :]
    listed = jnp.any(query_lists[:, :, None] + 1 == offsets[:, None, :], axis=1)
    inside = (lookup_segments >= 0) & (lookup_segments < block_total)
    inside_query = (query_blocks >= 0) & (query_blocks < block_total)
    allowed = (
        inside_query[:, None]
        & inside[None, :]
        & (query_docs[:, None] == key_docs[None, :])
        & ((offsets == 0) | listed)
    )
    expanded = jnp.repeat(jnp.repeat(allowed, BLK, axis=0), BLK, axis=1)
    within = jnp.arange(BLK, dtype=jnp.int32)
    asking_items = (query_blocks[:, None] * BLK + within[None, :]).reshape(-1)
    key_tokens = (lookup_segments[:, None] * BLK + within[None, :]).reshape(-1)
    return expanded & (asking_items[:, None] >= key_tokens[None, :])


def tile_forward(query_rows, key_rows, value_rows, visible):
    scaling = 1.0 / math.sqrt(query_rows.shape[-1])
    scores = (
        jnp.einsum("bnhd,bmhd->bhnm", query_rows, key_rows, preferred_element_type=jnp.float32)
        * scaling
    )
    scores = jnp.where(visible[:, None], scores, NEG_FILL)
    row_max = jnp.max(scores, axis=-1)
    raised = jnp.exp(scores - row_max[..., None])
    row_sum = jnp.sum(raised, axis=-1)
    weights = (raised / row_sum[..., None]).astype(jnp.bfloat16)
    output = jnp.einsum("bhnm,bmhd->bnhd", weights, value_rows, preferred_element_type=jnp.float32)
    return (output, row_max + jnp.log(row_sum))


def tile_backward(query_rows, key_rows, value_rows, visible, cotangent, logsum, deltas):
    scaling = 1.0 / math.sqrt(query_rows.shape[-1])
    scores = (
        jnp.einsum("bnhd,bmhd->bhnm", query_rows, key_rows, preferred_element_type=jnp.float32)
        * scaling
    )
    chances = jnp.where(visible[:, None], jnp.exp(scores - logsum[..., None]), 0.0)
    rounded = chances.astype(jnp.bfloat16)
    value_grad = jnp.einsum(
        "bhnm,bnhd->bmhd", rounded, cotangent, preferred_element_type=jnp.float32
    )
    chance_grad = jnp.einsum(
        "bnhd,bmhd->bhnm", cotangent, value_rows, preferred_element_type=jnp.float32
    )
    score_grad = (chances * (chance_grad - deltas[..., None])).astype(jnp.bfloat16)
    query_grad = (
        jnp.einsum("bhnm,bmhd->bnhd", score_grad, key_rows, preferred_element_type=jnp.float32)
        * scaling
    )
    key_grad = (
        jnp.einsum("bhnm,bnhd->bmhd", score_grad, query_rows, preferred_element_type=jnp.float32)
        * scaling
    )
    return (query_grad, key_grad, value_grad)


def softmax_forward(queries, key_input, value_input, document_ids, block_lists):
    length = queries.shape[0]
    head_count = queries.shape[1] // HD
    per_device = length // BLK
    margin = WB - 1
    reach_devices = (margin + per_device - 1) // per_device
    devices = lax.axis_size("ctx")
    position = lax.axis_index("ctx")
    block_total = per_device * devices
    key_rows = key_input.reshape(length, head_count, HD)
    value_rows = value_input.reshape(length, head_count, HD)
    fetched = []
    for distance in range(reach_devices, 0, -1):
        fetched.append(passed_along((key_rows, value_rows, document_ids), "ctx", distance))
    context_keys = jnp.concatenate([arrived[0] for arrived in fetched] + [key_rows], axis=0)
    context_values = jnp.concatenate([arrived[1] for arrived in fetched] + [value_rows], axis=0)
    context_docs = jnp.concatenate([arrived[2] for arrived in fetched] + [document_ids], axis=0)
    context_blocks = (position - reach_devices) * per_device + jnp.arange(
        (reach_devices + 1) * per_device, dtype=jnp.int32
    )
    own_blocks = position * per_device + jnp.arange(per_device, dtype=jnp.int32)
    starts = [reach_devices * per_device - margin]
    window_keys = jnp.stack([context_keys for window_start in starts])
    window_values = jnp.stack([context_values for window_start in starts])
    visible = jnp.stack(
        [
            token_visible(
                own_blocks, context_blocks, document_ids, context_docs, block_lists, block_total
            )
            for local_block, window_start in enumerate(starts)
        ]
    )
    query_blocks = queries.reshape(per_device, BLK, head_count, HD)
    output, logsum = tile_forward(query_blocks, window_keys, window_values, visible)
    rounded = output.astype(jnp.bfloat16)
    saved = (
        window_keys,
        window_values,
        visible,
        starts,
        reach_devices,
        own_blocks,
        block_total,
        key_rows,
        value_rows,
    )
    return (rounded, logsum, saved)


def softmax_backward(queries, cotangent, rounded, logsum, saved):
    (
        window_keys,
        window_values,
        visible,
        starts,
        reach_devices,
        own_blocks,
        block_total,
        key_rows,
        value_rows,
    ) = saved
    length = queries.shape[0]
    head_count = queries.shape[1] // HD
    per_device = length // BLK
    query_blocks = queries.reshape(per_device, BLK, head_count, HD)
    cot_blocks = cotangent.reshape(per_device, BLK, head_count, HD)
    deltas = jnp.sum(
        cot_blocks.astype(jnp.float32) * rounded.astype(jnp.float32), axis=-1
    ).transpose(0, 2, 1)
    query_grad, key_part, value_part = tile_backward(
        query_blocks, window_keys, window_values, visible, cot_blocks, logsum, deltas
    )
    flat_shape = (length, head_count * HD)
    key_acc = jnp.zeros(((reach_devices + 1) * length, head_count, HD), jnp.float32)
    value_acc = jnp.zeros(((reach_devices + 1) * length, head_count, HD), jnp.float32)
    for local_block, window_start in enumerate(starts):
        key_acc = key_acc.at[window_start * BLK : (window_start + WB) * BLK].add(
            key_part[local_block]
        )
        value_acc = value_acc.at[window_start * BLK : (window_start + WB) * BLK].add(
            value_part[local_block]
        )
    key_total = key_acc[reach_devices * length :]
    summed_vector_entry = value_acc[reach_devices * length :]
    for distance in range(1, reach_devices + 1):
        slot_index = reach_devices - distance
        incoming = (
            passed_along(
                key_acc[slot_index * length : (slot_index + 1) * length].astype(jnp.bfloat16),
                "ctx",
                -distance,
            ).astype(jnp.float32),
            passed_along(
                value_acc[slot_index * length : (slot_index + 1) * length].astype(jnp.bfloat16),
                "ctx",
                -distance,
            ).astype(jnp.float32),
        )
        key_total = key_total + incoming[0]
        summed_vector_entry = summed_vector_entry + incoming[1]
    return (
        query_grad.astype(jnp.bfloat16).reshape(flat_shape),
        key_total.astype(jnp.bfloat16).reshape(flat_shape),
        summed_vector_entry.astype(jnp.bfloat16).reshape(flat_shape),
    )


def stretch_parts(query_rows, key_rows, rate_rows):
    running = jnp.cumsum(rate_rows, axis=1)
    length = rate_rows.shape[1]
    order = jnp.arange(length, dtype=jnp.int32)
    causal = (order[:, None] >= order[None, :])[None]
    spread = running[:, :, None] - running[:, None, :]
    damping = jnp.where(causal, jnp.exp(jnp.where(causal, spread, 0.0)), 0.0)
    products = jnp.einsum("thd,jhd->htj", query_rows, key_rows, preferred_element_type=jnp.float32)
    mixing = (products * damping).astype(jnp.bfloat16)
    to_end = jnp.exp(running[:, -1:] - running)
    carry_out = jnp.exp(running[:, -1])
    return (running, damping, mixing, to_end, carry_out)


def combine_affine(earlier, later_part):
    return (earlier[0] * later_part[0], later_part[0][:, None, None] * earlier[1] + later_part[1])


def linear_part(queries, key_input, value_input, decay, gain, cotangent):
    length = queries.shape[0]
    head_count = queries.shape[1] // HD
    features = head_count * HD * lax.axis_size("head")
    query_rows = queries.reshape(length, head_count, HD)
    key_rows = key_input.reshape(length, head_count, HD)
    value_rows = value_input.reshape(length, head_count, HD)
    running, damping, mixing, to_end, carry_out = stretch_parts(query_rows, key_rows, decay)
    leave_factor = to_end.T[:, :, None]
    decay_in = jnp.exp(running).T[:, :, None]
    keys_scaled = (key_rows.astype(jnp.float32) * leave_factor).astype(jnp.bfloat16)
    update = jnp.einsum("jhd,jhe->hde", keys_scaled, value_rows, preferred_element_type=jnp.float32)
    identity = (jnp.ones((head_count,), jnp.float32), jnp.zeros((head_count, HD, HD), jnp.float32))
    state_in = prefix((carry_out, update), "ctx", combine_affine, identity, False)[1]
    state_half = state_in.astype(jnp.bfloat16)
    inner = jnp.einsum("htj,jhd->thd", mixing, value_rows, preferred_element_type=jnp.float32)
    raw_output = inner + decay_in * jnp.einsum(
        "thd,hde->the", query_rows, state_half, preferred_element_type=jnp.float32
    )
    gain_rows = gain.reshape(head_count, HD)
    scaled = cotangent.reshape(length, head_count, HD).astype(jnp.float32) * gain_rows
    squares_part = jnp.sum(raw_output * raw_output, axis=(1, 2))
    squares = lax.psum(squares_part, "head")
    root_mean = jnp.sqrt(squares / features + EPSILON)
    normalized = raw_output / root_mean[:, None, None]
    coefficient = lax.psum(jnp.sum(scaled * normalized, axis=(1, 2)), "head") / (
        features * root_mean
    )
    output = (raw_output / root_mean[:, None, None] * gain_rows).astype(jnp.bfloat16)
    raw_grads = (scaled - raw_output * coefficient[:, None, None]) / root_mean[:, None, None]
    grad_half = raw_grads.astype(jnp.bfloat16)
    queries_scaled = (query_rows.astype(jnp.float32) * decay_in).astype(jnp.bfloat16)
    back_terms = jnp.einsum(
        "thd,the->hde", queries_scaled, grad_half, preferred_element_type=jnp.float32
    )
    later_grad = prefix((carry_out, back_terms), "ctx", combine_affine, identity, True)[1]
    later_half = later_grad.astype(jnp.bfloat16)
    mix_grad = (
        jnp.einsum("thd,jhd->htj", grad_half, value_rows, preferred_element_type=jnp.float32)
        * damping
    ).astype(jnp.bfloat16)
    query_grad = jnp.einsum(
        "htj,jhd->thd", mix_grad, key_rows, preferred_element_type=jnp.float32
    ) + decay_in * jnp.einsum(
        "the,hde->thd", grad_half, state_half, preferred_element_type=jnp.float32
    )
    key_grad = jnp.einsum(
        "htj,thd->jhd", mix_grad, query_rows, preferred_element_type=jnp.float32
    ) + leave_factor * jnp.einsum(
        "jhe,hde->jhd", value_rows, later_half, preferred_element_type=jnp.float32
    )
    value_grad = jnp.einsum(
        "htj,thd->jhd", mixing, grad_half, preferred_element_type=jnp.float32
    ) + leave_factor * jnp.einsum(
        "jhd,hde->jhe", key_rows, later_half, preferred_element_type=jnp.float32
    )
    flat_shape = (length, head_count * HD)
    return (
        output.reshape(flat_shape),
        query_grad.astype(jnp.bfloat16).reshape(flat_shape),
        key_grad.astype(jnp.bfloat16).reshape(flat_shape),
        value_grad.astype(jnp.bfloat16).reshape(flat_shape),
    )


def body(
    softmax_query,
    softmax_key,
    softmax_value,
    document_ids,
    block_lists,
    linear_key,
    linear_value,
    linear_decay,
    linear_gain,
    linear_cotangent,
):
    rounded, logsum, saved = softmax_forward(
        softmax_query, softmax_key, softmax_value, document_ids, block_lists
    )
    flat_output = rounded.reshape(softmax_query.shape)
    linear_parts = linear_part(
        flat_output, linear_key, linear_value, linear_decay, linear_gain, linear_cotangent
    )
    soft_grads = softmax_backward(softmax_query, linear_parts[1], rounded, logsum, saved)
    return (
        flat_output,
        soft_grads[0],
        soft_grads[1],
        soft_grads[2],
        linear_parts[0],
        linear_parts[1],
        linear_parts[2],
        linear_parts[3],
    )


def solution(mesh):
    placed = (
        P("ctx", "head"),
        P("ctx", "head"),
        P("ctx", "head"),
        P("ctx"),
        P("ctx", None),
        P("ctx", "head"),
        P("ctx", "head"),
        P("head", "ctx"),
        P("head"),
        P("ctx", "head"),
    )
    return jax.shard_map(
        body,
        mesh=mesh,
        in_specs=placed,
        out_specs=(
            P("ctx", "head"),
            P("ctx", "head"),
            P("ctx", "head"),
            P("ctx", "head"),
            P("ctx", "head"),
            P("ctx", "head"),
            P("ctx", "head"),
            P("ctx", "head"),
        ),
        check_vma=False,
    )
```

profile of v0, /device:TPU:0, one launch (start us, length us, event | category | flops | bytes accessed | tf_op | source)
XLA Modules:
  0.0 201.1 jit_solution(15975443479351510149)
XLA Ops:
  7.2 1.0 copy.143
  10.4 5.4 %collective-permute-start.5 = (s32[1]{0:T(128)}, s32[1]{0:T(128)}, u32[]{:S(2)}, u32[]{:S(2)}) collective-permute-start(s32[1]{0:T(128)} %param.25), channel_id=1, source_target_pairs={{0,2},{2,4},{4,6},{6,8},{8,10},{10,12},{12,14},{14,16},{16,18},{18... | collective-permute-start | bytes 20 | tf_op jit(solution)/shard_map/ppermute | solution.py:20
  15.8 3.5 %collective-permute-start.4 = (s32[1]{0:T(128)}, s32[1]{0:T(128)}, u32[]{:S(2)}, u32[]{:S(2)}) collective-permute-start(s32[1]{0:T(128)} %param.25), channel_id=1, source_target_pairs={{0,4},{2,6},{4,8},{6,10},{8,12},{10,14},{12,16},{14,18},{16,20},{1... | collective-permute-start | bytes 20 | tf_op jit(solution)/shard_map/ppermute | solution.py:20
  19.3 4.4 %collective-permute-start.3 = (s32[1]{0:T(128)}, s32[1]{0:T(128)}, u32[]{:S(2)}, u32[]{:S(2)}) collective-permute-start(s32[1]{0:T(128)} %param.25), channel_id=1, source_target_pairs={{0,6},{2,8},{4,10},{6,12},{8,14},{10,16},{12,18},{14,20},{16,22},{... | collective-permute-start | bytes 20 | tf_op jit(solution)/shard_map/ppermute | solution.py:20
  23.7 1.0 copy.135
  24.8 2.5 %collective-permute-start.8 = (bf16[128,4,128]{2,0,1:T(8,128)(2,1)S(1)}, bf16[128,4,128]{2,0,1:T(8,128)(2,1)S(1)}, u32[]{:S(2)}, u32[]{:S(2)}) collective-permute-start(bf16[128,4,128]{2,0,1:T(8,128)(2,1)S(1)} %copy.136), channel_id=1, source_target_pairs={{0,2},{2,4},{4,6},{6,8},{8,10},{10,12},{12,14},{14,16},{16,18},{18... | collective-permute-start | bytes 393224 | tf_op jit(solution)/shard_map/ppermute | solution.py:20
  27.4 2.9 %collective-permute-start.7 = (bf16[128,4,128]{2,0,1:T(8,128)(2,1)S(1)}, bf16[128,4,128]{2,0,1:T(8,128)(2,1)S(1)}, u32[]{:S(2)}, u32[]{:S(2)}) collective-permute-start(bf16[128,4,128]{2,0,1:T(8,128)(2,1)S(1)} %copy.136), channel_id=1, source_target_pairs={{0,4},{2,6},{4,8},{6,10},{8,12},{10,14},{12,16},{14,18},{16,20},{1... | collective-permute-start | bytes 393224 | tf_op jit(solution)/shard_map/ppermute | solution.py:20
  30.9 1.0 copy.193
  31.9 1.0 copy.134
  33.0 1.2 dynamic-slice.10
  35.3 39.2 %all-reduce = bf16[64]{0:T(256)(128)(2,1)S(1)} all-reduce(bf16[64]{0:T(256)(128)(2,1)S(1)} %dynamic-update-slice.4), channel_id=2, replica_groups=mesh['ctx'=16,'head'=2] {'ctx'}, use_global_device_ids=true, to_apply=%add | all-reduce | flops 64 | bytes 256
  75.9 1.3 collective-permute-start.6
  77.2 2.4 %collective-permute-start.2 = (bf16[128,4,128]{0,2,1:T(8,128)(2,1)S(1)}, bf16[128,4,128]{0,2,1:T(8,128)(2,1)}, u32[]{:S(2)}, u32[]{:S(2)}) collective-permute-start(bf16[128,4,128]{0,2,1:T(8,128)(2,1)S(1)} %bitcast.219), channel_id=1, source_target_pairs={{0,2},{2,4},{4,6},{6,8},{8,10},{10,12},{12,14},{14,16},{16,18},{18... | collective-permute-start | bytes 393224 | tf_op jit(solution)/shard_map/ppermute | solution.py:20
  79.6 1.9 collective-permute-start.1
  81.5 2.0 %or_and_fusion = pred[4]{0:T(512)(128)(4,1)S(1)} fusion(pred[4]{0:T(512)(128)(4,1)S(1)} %compare_reduce_fusion, pred[]{:T(512)S(6)} %and.52, s32[1]{0:T(128)} %copy.225, s32[1]{0:T(128)} %collective-permute-done.5, s32[1]{0:T(128)} %collective-permute-done.4, s32[1]{0:T(128)} %collective-permute-done.3, s32[]{:T(128)} %bitcast.202, s32[]{:T(128)S(6)} %sub.86, ...), kind=kLoop, calls=%fused_computation.103 | loop fusion | flops 56 | bytes 37 | tf_op jit(solution)/shard_map/and | solution.py:52
  83.8 1.3 collective-permute-start
  85.7 1.9 collective-permute-done
  88.3 1.4 convolution_convert_fusion
  90.9 2.5 %psum.14 = f32[128]{0:T(128)S(1)} all-reduce(f32[128]{0:T(128)S(1)} %get-tuple-element.242), channel_id=1, replica_groups=mesh['ctx'=16,'head'=2] {'head'}, use_global_device_ids=true, to_apply=%region_7.8 | all-reduce | flops 128 | bytes 1024 | tf_op jit(solution)/shard_map/psum | solution.py:252
  93.6 2.5 %psum.15 = f32[128]{0:T(128)S(1)} all-reduce(f32[128]{0:T(128)S(1)} %multiply_reduce_fusion), channel_id=1, replica_groups=mesh['ctx'=16,'head'=2] {'head'}, use_global_device_ids=true, to_apply=%region_9.10 | all-reduce | flops 128 | bytes 1024 | tf_op jit(solution)/shard_map/psum | solution.py:255
  98.6 1.5 fusion.3
  102.0 1.3 fusion.61
  104.1 1.3 collective-permute-start.11
  105.4 1.3 collective-permute-start.10
  106.7 1.4 collective-permute-start.9
  108.1 1.3 fusion.62
  110.2 1.3 collective-permute-start.14
  111.5 1.3 collective-permute-start.13
  114.7 1.8 collective-permute-done.11
  116.6 1.3 collective-permute-start.12
  117.9 1.0 fusion.32
  119.8 4.8 %collective-permute-done.14 = bf16[128,4,128]{0,2,1:T(8,128)(2,1)S(1)} collective-permute-done((bf16[128,4,128]{0,2,1:T(8,128)(2,1)}, bf16[128,4,128]{0,2,1:T(8,128)(2,1)S(1)}, u32[]{:S(2)}, u32[]{:S(2)}) %collective-permute-start.14) | collective-permute-done | bytes 131104 | tf_op jit(solution)/shard_map/ppermute | solution.py:20
  126.4 50.0 %all-gather.8.cloned.1.call-done = bf16[64,128,128]{2,1,0:T(8,128)(2,1)} async-done(((bf16[4,128,128]{2,1,0:T(8,128)(2,1)}), bf16[64,128,128]{2,1,0:T(8,128)(2,1)}) %all-gather.8.cloned.1.call-update) | async-done | bytes 2097168 | tf_op jit(solution)/shard_map/all_gather | solution.py:28
  176.4 15.9 %while.31 = (s32[]{:T(128)}, f32[4,128,128]{2,1,0:T(8,128)S(1)}, s32[]{:T(128)}, bf16[16,4]{1,0:T(8,128)(2,1)S(1)}, bf16[16,4,128,128]{3,2,1,0:T(8,128)(2,1)}, /*index=5*/s32[]{:T(128)}, s32[]{:T(128)}, s32[]{:T(128)}, s32[]{:T(128)}) while((s32[]{:T(128)}, f32[4,128,128]{2,1,0:T(8,128)S(1)}, s32[]{:T(128)}, bf16[16,4]{1,0:T(8,128)(2,1)S(1)}, ...), condition=%wide.region_12.13_spmd, body=%wide.region_11.12_spmd.sunk | while | flops 196618 | bytes 655555 | solution.py:43
  176.4 1.0 convert_add_fusion.5
  177.5 1.0 convert_add_fusion.5
  178.5 1.0 convert_add_fusion.5
  179.6 1.0 convert_add_fusion.5
  180.7 1.0 convert_add_fusion.5
  181.7 1.0 convert_add_fusion.5
  182.8 1.0 convert_add_fusion.5
  183.8 1.0 convert_add_fusion.5
  184.9 1.0 convert_add_fusion.5
  186.0 1.0 convert_add_fusion.5
  187.0 1.0 convert_add_fusion.5
  188.1 1.0 convert_add_fusion.5
  189.1 1.0 convert_add_fusion.5
  190.2 1.0 convert_add_fusion.5
  (103 shorter events, 20.6 us)
Async XLA Ops:
  7.2 2.4 %copy-start = (bf16[128,512]{1,0:T(8,128)(2,1)S(1)}, bf16[128,512]{1,0:T(8,128)(2,1)}, u32[]{:S(2)}) copy-start(bf16[128,512]{1,0:T(8,128)(2,1)} %param.28) | copy-start | bytes 393220
  7.2 68.5 %copy-start.8 = (s32[1,2]{1,0:T(1,128)S(1)}, s32[1,2]{1,0:T(1,128)}, u32[]{:S(2)}) copy-start(s32[1,2]{1,0:T(1,128)} %param.26) | copy-start | bytes 28
  7.2 83.0 %all-gather.6.cloned.1.call-start = ((), (), s32[]{:S(2)}) async-start(), calls=%async_computation | async-start | bytes 2228224 | tf_op jit(solution)/shard_map/all_gather | solution.py:28
  10.4 166.0 %all-gather.8.cloned.1.call-start = ((), (), s32[]{:S(2)}) async-start(), calls=%async_computation.1 | async-start | bytes 2228224 | tf_op jit(solution)/shard_map/all_gather | solution.py:28
  10.4 65.4 %collective-permute-start.5 = (s32[1]{0:T(128)}, s32[1]{0:T(128)}, u32[]{:S(2)}, u32[]{:S(2)}) collective-permute-start(s32[1]{0:T(128)} %param.25), channel_id=1, source_target_pairs={{0,2},{2,4},{4,6},{6,8},{8,10},{10,12},{12,14},{14,16},{16,18},{18... | collective-permute-start | bytes 20 | tf_op jit(solution)/shard_map/ppermute | solution.py:20
  15.8 61.4 %collective-permute-start.4 = (s32[1]{0:T(128)}, s32[1]{0:T(128)}, u32[]{:S(2)}, u32[]{:S(2)}) collective-permute-start(s32[1]{0:T(128)} %param.25), channel_id=1, source_target_pairs={{0,4},{2,6},{4,8},{6,10},{8,12},{10,14},{12,16},{14,18},{16,20},{1... | collective-permute-start | bytes 20 | tf_op jit(solution)/shard_map/ppermute | solution.py:20
  19.3 60.3 %collective-permute-start.3 = (s32[1]{0:T(128)}, s32[1]{0:T(128)}, u32[]{:S(2)}, u32[]{:S(2)}) collective-permute-start(s32[1]{0:T(128)} %param.25), channel_id=1, source_target_pairs={{0,6},{2,8},{4,10},{6,12},{8,14},{10,16},{12,18},{14,20},{16,22},{... | collective-permute-start | bytes 20 | tf_op jit(solution)/shard_map/ppermute | solution.py:20
  24.8 59.0 %collective-permute-start.8 = (bf16[128,4,128]{2,0,1:T(8,128)(2,1)S(1)}, bf16[128,4,128]{2,0,1:T(8,128)(2,1)S(1)}, u32[]{:S(2)}, u32[]{:S(2)}) collective-permute-start(bf16[128,4,128]{2,0,1:T(8,128)(2,1)S(1)} %copy.136), channel_id=1, source_target_pairs={{0,2},{2,4},{4,6},{6,8},{8,10},{10,12},{12,14},{14,16},{16,18},{18... | collective-permute-start | bytes 393224 | tf_op jit(solution)/shard_map/ppermute | solution.py:20
  27.4 57.8 %collective-permute-start.7 = (bf16[128,4,128]{2,0,1:T(8,128)(2,1)S(1)}, bf16[128,4,128]{2,0,1:T(8,128)(2,1)S(1)}, u32[]{:S(2)}, u32[]{:S(2)}) collective-permute-start(bf16[128,4,128]{2,0,1:T(8,128)(2,1)S(1)} %copy.136), channel_id=1, source_target_pairs={{0,4},{2,6},{4,8},{6,10},{8,12},{10,14},{12,16},{14,18},{16,20},{1... | collective-permute-start | bytes 393224 | tf_op jit(solution)/shard_map/ppermute | solution.py:20
  75.9 9.3 %collective-permute-start.6 = (bf16[128,4,128]{2,0,1:T(8,128)(2,1)S(1)}, bf16[128,4,128]{2,0,1:T(8,128)(2,1)S(1)}, u32[]{:S(2)}, u32[]{:S(2)}) collective-permute-start(bf16[128,4,128]{2,0,1:T(8,128)(2,1)S(1)} %copy.136), channel_id=1, source_target_pairs={{0,6},{2,8},{4,10},{6,12},{8,14},{10,16},{12,18},{14,20},{16,22},{... | collective-permute-start | bytes 393224 | tf_op jit(solution)/shard_map/ppermute | solution.py:20
  77.2 8.5 %collective-permute-start.2 = (bf16[128,4,128]{0,2,1:T(8,128)(2,1)S(1)}, bf16[128,4,128]{0,2,1:T(8,128)(2,1)}, u32[]{:S(2)}, u32[]{:S(2)}) collective-permute-start(bf16[128,4,128]{0,2,1:T(8,128)(2,1)S(1)} %bitcast.219), channel_id=1, source_target_pairs={{0,2},{2,4},{4,6},{6,8},{8,10},{10,12},{12,14},{14,16},{16,18},{18... | collective-permute-start | bytes 393224 | tf_op jit(solution)/shard_map/ppermute | solution.py:20
  79.6 6.1 %collective-permute-start.1 = (bf16[128,4,128]{0,2,1:T(8,128)(2,1)S(1)}, bf16[128,4,128]{0,2,1:T(8,128)(2,1)}, u32[]{:S(2)}, u32[]{:S(2)}) collective-permute-start(bf16[128,4,128]{0,2,1:T(8,128)(2,1)S(1)} %bitcast.220), channel_id=1, source_target_pairs={{0,4},{2,6},{4,8},{6,10},{8,12},{10,14},{12,16},{14,18},{16,20},{1... | collective-permute-start | bytes 393224 | tf_op jit(solution)/shard_map/ppermute | solution.py:20
  83.8 14.8 %copy-start.1 = (pred[128,512]{0,1:T(8,128)(4,1)}, pred[128,512]{0,1:T(8,128)(4,1)S(1)}, u32[]{:S(2)}) copy-start(pred[128,512]{0,1:T(8,128)(4,1)S(1)} %compare_and_fusion) | copy-start | bytes 196612
  83.8 3.8 %collective-permute-start = (bf16[128,4,128]{0,2,1:T(8,128)(2,1)S(1)}, bf16[128,4,128]{0,2,1:T(8,128)(2,1)S(1)}, u32[]{:S(2)}, u32[]{:S(2)}) collective-permute-start(bf16[128,4,128]{0,2,1:T(8,128)(2,1)S(1)} %bitcast.221), channel_id=1, source_target_pairs={{0,6},{2,8},{4,10},{6,12},{8,14},{10,16},{12,18},{14,20},{16,22},{... | collective-permute-start | bytes 393224 | tf_op jit(solution)/shard_map/ppermute | solution.py:20
  87.6 0.7 copy-start.7
  89.9 0.7 copy-start.4
  90.6 2.8 %copy-start.6 = (f32[512]{0:T(512)S(1)}, f32[512]{0:T(512)}, u32[]{:S(2)}) copy-start(f32[512]{0:T(512)} %param.30) | copy-start | bytes 6148
  100.0 0.8 copy-start.3
  101.2 6.9 %copy-start.2 = (pred[128,512]{0,1:T(8,128)(4,1)S(1)}, pred[128,512]{0,1:T(8,128)(4,1)}, u32[]{:S(2)}) copy-start(pred[128,512]{0,1:T(8,128)(4,1)} %copy-done.1) | copy-start | bytes 196612
  104.1 12.5 %collective-permute-start.11 = (bf16[128,4,128]{2,0,1:T(8,128)(2,1)}, bf16[128,4,128]{2,0,1:T(8,128)(2,1)S(1)}, u32[]{:S(2)}, u32[]{:S(2)}) collective-permute-start(bf16[128,4,128]{2,0,1:T(8,128)(2,1)} %get-tuple-element.234), channel_id=1, source_target_pairs={{6,0},{8,2},{10,4},{12,6},{14,8},{16,10},{18,12},{20,14},{22,16},{... | collective-permute-start | bytes 393224 | tf_op jit(solution)/shard_map/ppermute | solution.py:20
  105.4 12.5 %collective-permute-start.10 = (bf16[128,4,128]{2,0,1:T(8,128)(2,1)}, bf16[128,4,128]{2,0,1:T(8,128)(2,1)}, u32[]{:S(2)}, u32[]{:S(2)}) collective-permute-start(bf16[128,4,128]{2,0,1:T(8,128)(2,1)} %get-tuple-element.235), channel_id=1, source_target_pairs={{4,0},{6,2},{8,4},{10,6},{12,8},{14,10},{16,12},{18,14},{20,16},{2... | collective-permute-start | bytes 393224 | tf_op jit(solution)/shard_map/ppermute | solution.py:20
  106.7 7.8 %copy-start.5 = (bf16[4,128,128]{2,1,0:T(8,128)(2,1)S(1)}, bf16[4,128,128]{2,1,0:T(8,128)(2,1)}, u32[]{:S(2)}) copy-start(bf16[4,128,128]{2,1,0:T(8,128)(2,1)} %copy-done.4) | copy-start | bytes 393220
  106.7 11.2 %collective-permute-start.9 = (bf16[128,4,128]{2,0,1:T(8,128)(2,1)}, bf16[128,4,128]{2,0,1:T(8,128)(2,1)}, u32[]{:S(2)}, u32[]{:S(2)}) collective-permute-start(bf16[128,4,128]{2,0,1:T(8,128)(2,1)} %get-tuple-element.233), channel_id=1, source_target_pairs={{2,0},{4,2},{6,4},{8,6},{10,8},{12,10},{14,12},{16,14},{18,16},{20... | collective-permute-start | bytes 393224 | tf_op jit(solution)/shard_map/ppermute | solution.py:20
  110.2 14.4 %collective-permute-start.14 = (bf16[128,4,128]{0,2,1:T(8,128)(2,1)}, bf16[128,4,128]{0,2,1:T(8,128)(2,1)S(1)}, u32[]{:S(2)}, u32[]{:S(2)}) collective-permute-start(bf16[128,4,128]{0,2,1:T(8,128)(2,1)} %get-tuple-element.231), channel_id=1, source_target_pairs={{6,0},{8,2},{10,4},{12,6},{14,8},{16,10},{18,12},{20,14},{22,16},{... | collective-permute-start | bytes 393224 | tf_op jit(solution)/shard_map/ppermute | solution.py:20
  111.5 13.1 %collective-permute-start.13 = (bf16[128,4,128]{0,2,1:T(8,128)(2,1)S(1)}, bf16[128,4,128]{0,2,1:T(8,128)(2,1)S(1)}, u32[]{:S(2)}, u32[]{:S(2)}) collective-permute-start(bf16[128,4,128]{0,2,1:T(8,128)(2,1)S(1)} %get-tuple-element.232), channel_id=1, source_target_pairs={{4,0},{6,2},{8,4},{10,6},{12,8},{14,10},{16,12},{18,14},{20,16},{2... | collective-permute-start | bytes 393224 | tf_op jit(solution)/shard_map/ppermute | solution.py:20
  116.6 8.0 %collective-permute-start.12 = (bf16[128,4,128]{0,2,1:T(8,128)(2,1)S(1)}, bf16[128,4,128]{0,2,1:T(8,128)(2,1)S(1)}, u32[]{:S(2)}, u32[]{:S(2)}) collective-permute-start(bf16[128,4,128]{0,2,1:T(8,128)(2,1)S(1)} %get-tuple-element.230), channel_id=1, source_target_pairs={{2,0},{4,2},{6,4},{8,6},{10,8},{12,10},{14,12},{16,14},{18,16},{20... | collective-permute-start | bytes 393224 | tf_op jit(solution)/shard_map/ppermute | solution.py:20
Sparse Core Ops, SparseCore 0:
  11.4 66.5 all-gather.5
  97.2 79.0 all-gather.7
where the time goes:
time: 202 us; the launch traced here: 201 us
  waiting for transfers between devices  58.6 us (29%)
  blocking collectives  44.2 us (22%)
  starting transfers between devices  33.4 us (17%)
  other arithmetic  21.7 us (11%)
  local copies, waits for them, and re-layouts  16.8 us (8%)
  between operations  15.8 us (8%)
  matrix products  10.2 us (5%)
    all_gather x2, waiting for transfers between devices, prefix(): lax.all_gather(a.astype(kind), axis)  50 us
    unnamed x1, blocking collectives  39.2 us
    ppermute x15, starting transfers between devices, passed_along(): return lax.ppermute(array, axis, pairs)  33.3 us
    add x15, other arithmetic, combine_affine(): later_part[0][:, None, None] * earlier[1] + later_part[1]  15.3 us
    unnamed x32, local copies, waits for them, and re-layouts  12.6 us
    ppermute x15, waiting for transfers between devices, passed_along(): return lax.ppermute(array, axis, pairs)  8.55 us
  transfers between devices with their start and end apart: 17, of which 4 were waited for; matrix products, arithmetic and copies ran while one was open for 12% of the time, Pallas kernels for 0%

commit v1 on v0

v1 whole, which is shorter than its diff:
```python
import functools
import math

import jax
import jax.numpy as jnp
from jax import lax
from jax.experimental import pallas as pl
from jax.experimental.pallas import tpu as pltpu
from jax.sharding import PartitionSpec as P

HD = 128
BLK = 128
REACH = 3
NEG = -1e30
EPSILON = 1e-05
MESH = pl.DeviceIdType.MESH
F32 = jnp.float32
BF16 = jnp.bfloat16


def dot(a, b, contract, precision=None):
    return lax.dot_general(
        a, b, (contract, ((), ())), precision=precision, preferred_element_type=F32
    )


def nn(a, b):
    return dot(a, b, ((1,), (0,)))


def nt(a, b):
    return dot(a, b, ((1,), (1,)))


def tn(a, b):
    return dot(a, b, ((0,), (0,)))


def kernel(
    n,
    groups,
    q_ref,
    k_ref,
    v_ref,
    doc_ref,
    list_ref,
    lk_ref,
    lv_ref,
    decay_ref,
    gain_ref,
    cot_ref,
    out_ref,
    dq_ref,
    dk_ref,
    dv_ref,
    lout_ref,
    lqg_ref,
    lkg_ref,
    lvg_ref,
    kbuf,
    vbuf,
    qbuf,
    gbuf,
    info,
    info_left,
    info_right,
    side,
    sidebuf,
    score,
    up_send,
    up_recv,
    state_send,
    state_recv,
    back_send,
    back_recv,
    later_send,
    later_recv,
    sums,
    sums_recv,
    near_send,
    near_recv,
    far_send,
    far_recv,
    head_send,
    head_recv,
):
    me = lax.axis_index("ctx")
    group = lax.axis_index("head")
    heads = q_ref.shape[1] // HD
    rows = heads * HD // n
    scaling = 1.0 / math.sqrt(HD)
    cols = [slice(h * HD, (h + 1) * HD) for h in range(heads)]

    barrier = pltpu.get_barrier_semaphore()

    def greet(o, c):
        pl.semaphore_signal(
            barrier, inc=1, device_id={"ctx": lax.rem(me + o, n)}, device_id_type=MESH
        )
        return c

    lax.fori_loop(1, n, greet, 0)
    for o in range(1, groups):
        pl.semaphore_signal(
            barrier, inc=1, device_id={"head": lax.rem(group + o, groups)}, device_id_type=MESH
        )

    def spread(src, dst, lane):
        def one(o, c):
            j = lax.rem(me + o, n)
            pltpu.make_async_remote_copy(
                src_ref=src.at[j],
                dst_ref=dst.at[me],
                send_sem=far_send.at[lane, j],
                recv_sem=far_recv.at[lane, me],
                device_id={"ctx": j},
                device_id_type=MESH,
            ).start()
            return c

        lax.fori_loop(1, n, one, 0)
        dst[me] = src[me]

    def collect(src, dst, lane):
        def one(o, c):
            j = lax.rem(me + n - o, n)
            pltpu.make_async_remote_copy(
                src_ref=src.at[j],
                dst_ref=dst.at[j],
                send_sem=far_send.at[lane, j],
                recv_sem=far_recv.at[lane, j],
                device_id={"ctx": j},
                device_id_type=MESH,
            ).wait()
            return c

        lax.fori_loop(1, n, one, 0)

    def near(kind, d, src, dst, step):
        return pltpu.make_async_remote_copy(
            src_ref=src,
            dst_ref=dst.at[d],
            send_sem=near_send.at[kind, d],
            recv_sem=near_recv.at[kind, d],
            device_id={"ctx": lax.rem(me + step + n, n)},
            device_id_type=MESH,
        )

    def send_near(kind, src, dst, way):
        for d in range(1, REACH + 1):
            target = me + way * d

            @pl.when((target >= 0) & (target < n))
            def _():
                near(kind, d, src, dst, way * d).start()

    def wait_near(kind, src, dst, way):
        for d in range(1, REACH + 1):
            target = me + way * d
            source = me - way * d

            @pl.when((target >= 0) & (target < n))
            def _():
                near(kind, d, src, dst, way * d).wait_send()

            @pl.when((source >= 0) & (source < n))
            def _():
                near(kind, d, src, dst, way * d).wait_recv()

    row_at = lax.broadcasted_iota(jnp.int32, (BLK, BLK), 0)
    col_at = lax.broadcasted_iota(jnp.int32, (BLK, BLK), 1)
    lower = (row_at >= col_at).astype(F32)
    rates = decay_ref[...]
    exact = lax.Precision.HIGHEST
    run_col = dot(lower, rates, ((1,), (1,)), exact)
    run_row = dot(rates, lower, ((1,), (1,)), exact)
    last = dot(rates, jnp.ones((BLK, BLK), F32), ((1,), (0,)), exact)
    carry = jnp.exp(last)
    causal = row_at >= col_at

    at_col = [jnp.broadcast_to(run_col[:, h : h + 1], (BLK, HD)) for h in range(heads)]
    leave = [jnp.exp(last[h : h + 1, :] - at_col[h]) for h in range(heads)]
    enter = [jnp.exp(at_col[h]) for h in range(heads)]
    damping = [
        jnp.where(causal, jnp.exp(jnp.where(causal, at_col[h] - run_row[h : h + 1, :], 0.0)), 0.0)
        for h in range(heads)
    ]
    updates = [
        tn((lk_ref[:, cols[h]].astype(F32) * leave[h]).astype(BF16), lv_ref[:, cols[h]])
        for h in range(heads)
    ]
    ext = up_send.shape[1] - rows
    high = carry.astype(BF16).astype(F32)
    low = carry - high
    ext_at = lax.broadcasted_iota(jnp.int32, (ext, HD), 0)
    tails = [
        jnp.where(ext_at < ext // 2, high[h : h + 1, :], low[h : h + 1, :]) for h in range(heads)
    ]
    per_head = n // heads
    for h in range(heads):
        for j in range(per_head):
            piece = jnp.concatenate([updates[h][j * rows : (j + 1) * rows], tails[h]], axis=0)
            up_send[h * per_head + j] = piece.astype(BF16)

    doc = doc_ref[0].astype(F32)
    first = list_ref[0, 0].astype(F32)
    second = list_ref[0, 1].astype(F32)
    info_at = lax.broadcasted_iota(jnp.int32, (8, HD), 0)
    info[...] = jnp.where(info_at == 0, doc, jnp.where(info_at == 1, first, second))
    kbuf[0] = k_ref[...]
    vbuf[0] = v_ref[...]
    qbuf[0] = q_ref[...]
    for d in range(1, REACH + 1):

        @pl.when(me - d < 0)
        def _():
            kbuf[d] = jnp.zeros_like(kbuf[d])
            vbuf[d] = jnp.zeros_like(vbuf[d])
            info_left[d] = jnp.full((8, HD), -1.0, F32)

        @pl.when(me + d >= n)
        def _():
            qbuf[d] = jnp.zeros_like(qbuf[d])
            gbuf[d] = jnp.zeros_like(gbuf[d])
            sidebuf[d] = jnp.zeros((8, HD), F32)
            info_right[d] = jnp.full((8, HD), -1.0, F32)

    pl.semaphore_wait(barrier, n - 1 + groups - 1)

    spread(up_send, up_recv, 0)
    send_near(0, info, info_left, 1)
    send_near(1, k_ref, kbuf, 1)
    send_near(2, v_ref, vbuf, 1)
    send_near(3, info, info_right, -1)

    collect(up_send, up_recv, 0)

    def carry_of(p):
        tail = up_recv[p, rows:, :].astype(F32)
        return tail[0:1, :] + tail[ext // 2 : ext // 2 + 1, :]

    def forward(p, state):
        state_send[p] = state.astype(BF16)
        return carry_of(p) * state + up_recv[p, :rows, :].astype(F32)

    lax.fori_loop(0, n, forward, jnp.zeros((rows, HD), F32))
    spread(state_send, state_recv, 1)

    wait_near(0, info, info_left, 1)
    wait_near(1, k_ref, kbuf, 1)
    bias = [jnp.where(causal, 0.0, NEG)]
    for d in range(1, REACH + 1):
        listed = (jnp.full((1, HD), first) == d - 1.0) | (jnp.full((1, HD), second) == d - 1.0)
        seen = (info_left[d][0:1, :] == doc) & listed
        bias.append(jnp.broadcast_to(jnp.where(seen, 0.0, NEG), (BLK, HD)))
    bias = jnp.concatenate(bias, axis=1)
    weights = []
    logsum = []
    for h in range(heads):
        keys = kbuf[:, :, cols[h]].reshape(-1, HD)
        s = nt(q_ref[:, cols[h]], keys) * scaling + bias
        score[h] = s
        m = jnp.max(s, axis=1, keepdims=True)
        e = jnp.exp(s - m)
        total = jnp.sum(e, axis=1, keepdims=True)
        weights.append((e / total).astype(BF16))
        logsum.append(m + jnp.log(total))
    wait_near(2, v_ref, vbuf, 1)
    send_near(4, q_ref, qbuf, -1)
    outs = []
    for h in range(heads):
        o = nn(weights[h], vbuf[:, :, cols[h]].reshape(-1, HD)).astype(BF16)
        outs.append(o)
        out_ref[:, cols[h]] = o

    mixing = [
        (nt(outs[h], lk_ref[:, cols[h]]) * damping[h]).astype(BF16) for h in range(heads)
    ]
    inner = [nn(mixing[h], lv_ref[:, cols[h]]) for h in range(heads)]
    collect(state_send, state_recv, 1)
    states = state_recv[...].astype(F32).reshape(heads * HD, HD).astype(BF16)
    raws = []
    scaled = []
    squares = jnp.zeros((BLK, HD), F32)
    cross = jnp.zeros((BLK, HD), F32)
    for h in range(heads):
        raw = inner[h] + enter[h] * nn(outs[h], states[h * HD : (h + 1) * HD])
        sc = cot_ref[:, cols[h]].astype(F32) * gain_ref[:, cols[h]]
        squares += raw * raw
        cross += sc * raw
        raws.append(raw)
        scaled.append(sc)
    sums[...] = jnp.where(
        col_at < HD // 2,
        jnp.sum(squares, axis=1, keepdims=True),
        jnp.sum(cross, axis=1, keepdims=True),
    )

    def to_head(o):
        return pltpu.make_async_remote_copy(
            src_ref=sums,
            dst_ref=sums_recv.at[o],
            send_sem=head_send.at[o],
            recv_sem=head_recv.at[o],
            device_id={"head": lax.rem(group + o, groups)},
            device_id_type=MESH,
        )

    for o in range(1, groups):
        to_head(o).start()
    qscaled = [(outs[h].astype(F32) * enter[h]).astype(BF16) for h in range(heads)]
    total = sums[...]
    for o in range(1, groups):
        to_head(o).wait()
        total = total + sums_recv[o]
    features = heads * HD * groups
    mean = jnp.broadcast_to(total[:, 0:1], (BLK, HD)) / features + EPSILON
    inverse = lax.rsqrt(mean)
    factor = jnp.broadcast_to(total[:, HD // 2 : HD // 2 + 1], (BLK, HD)) / (features * mean)
    halves = [((scaled[h] - raws[h] * factor) * inverse).astype(BF16) for h in range(heads)]
    mix_grads = []
    deltas = []
    for h in range(heads):
        mg = (nt(halves[h], lv_ref[:, cols[h]]) * damping[h]).astype(BF16)
        mix_grads.append(mg)
        g = nn(mg, lk_ref[:, cols[h]]) + enter[h] * nt(halves[h], states[h * HD : (h + 1) * HD])
        g = g.astype(BF16)
        lqg_ref[:, cols[h]] = g
        gbuf[0, :, cols[h]] = g
        deltas.append(
            jnp.sum(g.astype(F32) * outs[h].astype(F32), axis=1, keepdims=True)
        )
    block = jnp.zeros((BLK, HD), F32)
    for h in range(heads):
        block = jnp.where(col_at == h, logsum[h], block)
        block = jnp.where(col_at == heads + h, deltas[h], block)
    side[...] = block.T[0 : 2 * heads, :]
    sidebuf[0] = side[...]
    send_near(5, gbuf.at[0], gbuf, -1)
    send_near(6, side, sidebuf, -1)
    for h in range(heads):
        back = tn(qscaled[h], halves[h])
        for j in range(per_head):
            back_send[h * per_head + j] = back[j * rows : (j + 1) * rows].astype(BF16)
    spread(back_send, back_recv, 2)

    for h in range(heads):
        lout_ref[:, cols[h]] = (raws[h] * inverse * gain_ref[:, cols[h]]).astype(BF16)
    for h in range(heads):
        chance = jnp.exp(score[h] - logsum[h])
        cg = nt(gbuf[0, :, cols[h]], vbuf[:, :, cols[h]].reshape(-1, HD))
        sg = (chance * (cg - deltas[h])).astype(BF16)
        keys = kbuf[:, :, cols[h]].reshape(-1, HD)
        dq_ref[:, cols[h]] = (nn(sg, keys) * scaling).astype(BF16)

    collect(back_send, back_recv, 2)

    def backward(i, state):
        p = n - 1 - i
        later_send[p] = state.astype(BF16)
        return carry_of(p) * state + back_recv[p].astype(F32)

    lax.fori_loop(0, n, backward, jnp.zeros((rows, HD), F32))
    spread(later_send, later_recv, 3)
    key_local = [tn(mix_grads[h], outs[h]) for h in range(heads)]
    value_local = [tn(mixing[h], halves[h]) for h in range(heads)]

    wait_near(3, info, info_right, -1)
    wait_near(4, q_ref, qbuf, -1)
    bias = [jnp.where(row_at <= col_at, 0.0, NEG)]
    for d in range(1, REACH + 1):
        theirs = info_right[d]
        listed = (theirs[1:2, :] == d - 1.0) | (theirs[2:3, :] == d - 1.0)
        seen = (theirs[0:1, :] == doc) & listed
        bias.append(jnp.broadcast_to(jnp.where(seen, 0.0, NEG), (BLK, HD)))
    bias = jnp.concatenate(bias, axis=1)
    wait_near(5, gbuf.at[0], gbuf, -1)
    wait_near(6, side, sidebuf, -1)
    for h in range(heads):
        queries = qbuf[:, :, cols[h]].reshape(-1, HD)
        grads = gbuf[:, :, cols[h]].reshape(-1, HD)
        logs = jnp.concatenate([sidebuf[d, h : h + 1, :] for d in range(REACH + 1)], axis=1)
        dels = jnp.concatenate(
            [sidebuf[d, heads + h : heads + h + 1, :] for d in range(REACH + 1)], axis=1
        )
        chance = jnp.exp(nt(k_ref[:, cols[h]], queries) * scaling + bias - logs)
        dv_ref[:, cols[h]] = nn(chance.astype(BF16), grads).astype(BF16)
        cg = nt(v_ref[:, cols[h]], grads)
        sg = (chance * (cg - dels)).astype(BF16)
        dk_ref[:, cols[h]] = (nn(sg, queries) * scaling).astype(BF16)

    collect(later_send, later_recv, 3)
    laters = later_recv[...].astype(F32).reshape(heads * HD, HD).astype(BF16)
    for h in range(heads):
        later = laters[h * HD : (h + 1) * HD]
        lkg_ref[:, cols[h]] = (
            key_local[h] + leave[h] * nt(lv_ref[:, cols[h]], later)
        ).astype(BF16)
        lvg_ref[:, cols[h]] = (
            value_local[h] + leave[h] * nn(lk_ref[:, cols[h]], later)
        ).astype(BF16)


def body(
    softmax_query,
    softmax_key,
    softmax_value,
    document_ids,
    block_lists,
    linear_key,
    linear_value,
    linear_decay,
    linear_gain,
    linear_cotangent,
):
    n = lax.axis_size("ctx")
    groups = lax.axis_size("head")
    length, width = softmax_query.shape
    heads = width // HD
    rows = heads * HD // n
    ext = 16 if rows % 16 == 0 else 8
    vmem = pl.BlockSpec(memory_space=pltpu.VMEM)
    smem = pl.BlockSpec(memory_space=pltpu.SMEM)
    slots = REACH + 1
    window = pltpu.VMEM((slots, length, width), BF16)
    part = pltpu.VMEM((n, rows, HD), BF16)
    return pl.pallas_call(
        functools.partial(kernel, n, groups),
        out_shape=[jax.ShapeDtypeStruct((length, width), BF16)] * 8,
        in_specs=[vmem, vmem, vmem, smem, smem, vmem, vmem, vmem, vmem, vmem],
        out_specs=[vmem] * 8,
        scratch_shapes=[
            window,
            window,
            window,
            window,
            pltpu.VMEM((8, HD), F32),
            pltpu.VMEM((slots, 8, HD), F32),
            pltpu.VMEM((slots, 8, HD), F32),
            pltpu.VMEM((2 * heads, HD), F32),
            pltpu.VMEM((slots, 2 * heads, HD), F32),
            pltpu.VMEM((heads, length, slots * HD), F32),
            pltpu.VMEM((n, rows + ext, HD), BF16),
            pltpu.VMEM((n, rows + ext, HD), BF16),
            part,
            part,
            part,
            part,
            part,
            part,
            pltpu.VMEM((length, HD), F32),
            pltpu.VMEM((groups, length, HD), F32),
            pltpu.SemaphoreType.DMA((7, slots)),
            pltpu.SemaphoreType.DMA((7, slots)),
            pltpu.SemaphoreType.DMA((4, n)),
            pltpu.SemaphoreType.DMA((4, n)),
            pltpu.SemaphoreType.DMA((groups,)),
            pltpu.SemaphoreType.DMA((groups,)),
        ],
        compiler_params=pltpu.CompilerParams(
            collective_id=0, has_side_effects=True, vmem_limit_bytes=32 * 1024 * 1024
        ),
    )(
        softmax_query,
        softmax_key,
        softmax_value,
        document_ids,
        block_lists,
        linear_key,
        linear_value,
        linear_decay,
        linear_gain.reshape(1, width),
        linear_cotangent,
    )


def solution(mesh):
    tokens = P("ctx", "head")
    return jax.shard_map(
        body,
        mesh=mesh,
        in_specs=(
            tokens,
            tokens,
            tokens,
            P("ctx"),
            P("ctx", None),
            tokens,
            tokens,
            P("head", "ctx"),
            P("head"),
            tokens,
        ),
        out_specs=(tokens,) * 8,
        check_vma=False,
    )
```

time: 202 us -> 70.5 us (0.35)
  waiting for transfers between devices: 58.6 us -> 0 us
  Pallas kernels: 0 us -> 56.9 us
  blocking collectives: 44.2 us -> 0 us
  starting transfers between devices: 33.4 us -> 0 us
  other arithmetic: 21.7 us -> 0 us
  between operations: 15.8 us -> 1.34 us
  matrix products: 10.2 us -> 0 us
  local copies, waits for them, and re-layouts: 16.8 us -> 12 us
    pallas_call x0 -> x1, Pallas kernels: none -> 56.9 us  [body(): pl.pallas_call(functools.partial(kernel, n, groups), out_shape=[jax.Shape...]
    all_gather x2 -> x0, waiting for transfers between devices: 50 us -> none  [prefix(): lax.all_gather(a.astype(kind), axis)]
    unnamed x1 -> x0, blocking collectives: 39.2 us -> none
    ppermute x15 -> x0, starting transfers between devices: 33.3 us -> none  [passed_along(): return lax.ppermute(array, axis, pairs)]
    add x19 -> x0, other arithmetic: 15.4 us -> none  [the longest x15 15.3 us: combine_affine(): later_part[0][:, None, None] * earlier[1] + later_part[1]]
    dot_general x18 -> x0, matrix products: 10.2 us -> none  [the longest x1 1.49 us: tile_backward(): jnp.einsum('bnhd,bmhd->bhnm', cotangent, value_rows, preferred_element_ty...]
    ppermute x15 -> x0, waiting for transfers between devices: 8.55 us -> none  [passed_along(): return lax.ppermute(array, axis, pairs)]
    psum x2 -> x0, blocking collectives: 4.93 us -> none  [the longest x1 2.47 us: linear_part(): lax.psum(jnp.sum(scaled * normalized, axis=(1, 2)), 'head')]
  transfers between devices with their start and end apart: 17 -> 0, of which waited for: 4 -> 0; matrix products, arithmetic and copies ran while one was open for 12% -> 0% of each run, Pallas kernels for 0% -> 0%
where the time goes in v1:
time: 70.5 us; the launch traced here: 70.3 us
  Pallas kernels  56.9 us (81%)
  local copies, waits for them, and re-layouts  12 us (17%)
  between operations  1.34 us (2%)
    pallas_call x1, Pallas kernels, body(): pl.pallas_call(functools.partial(kernel, n, groups), out_shape=[jax.Shape...  56.9 us
    unnamed x26, local copies, waits for them, and re-layouts  12 us

profile of v1, /device:TPU:0, one launch (start us, length us, event | category | flops | bytes accessed | tf_op | source)
XLA Modules:
  0.0 70.3 jit_solution(6470597734773744950)
XLA Ops:
  0.6 0.0 copy-start.6
  1.3 0.0 copy-start.8
  1.3 0.0 copy-done.6
  1.3 0.6 copy-done.8
  2.0 0.0 copy-start
  2.0 0.9 %copy-done = bf16[128,512]{1,0:T(8,128)(2,1)S(1)} copy-done((bf16[128,512]{1,0:T(8,128)(2,1)S(1)}, bf16[128,512]{1,0:T(8,128)(2,1)}, u32[]{:S(2)}) %copy-start) | copy-done | bytes 131096
  2.9 0.0 copy-start.1
  2.9 0.9 %copy-done.1 = bf16[128,512]{1,0:T(8,128)(2,1)S(1)} copy-done((bf16[128,512]{1,0:T(8,128)(2,1)S(1)}, bf16[128,512]{1,0:T(8,128)(2,1)}, u32[]{:S(2)}) %copy-start.1) | copy-done | bytes 131096
  3.8 0.0 copy-start.2
  3.8 0.9 %copy-done.2 = bf16[128,512]{1,0:T(8,128)(2,1)S(1)} copy-done((bf16[128,512]{1,0:T(8,128)(2,1)S(1)}, bf16[128,512]{1,0:T(8,128)(2,1)}, u32[]{:S(2)}) %copy-start.2) | copy-done | bytes 131096
  4.7 0.0 copy-start.3
  4.7 0.9 %copy-done.3 = bf16[128,512]{1,0:T(8,128)(2,1)S(1)} copy-done((bf16[128,512]{1,0:T(8,128)(2,1)S(1)}, bf16[128,512]{1,0:T(8,128)(2,1)}, u32[]{:S(2)}) %copy-start.3) | copy-done | bytes 131096
  5.6 0.0 copy-start.4
  5.6 0.9 %copy-done.4 = bf16[128,512]{1,0:T(8,128)(2,1)S(1)} copy-done((bf16[128,512]{1,0:T(8,128)(2,1)S(1)}, bf16[128,512]{1,0:T(8,128)(2,1)}, u32[]{:S(2)}) %copy-start.4) | copy-done | bytes 131096
  6.5 0.0 copy-start.5
  6.5 0.9 %copy-done.5 = bf16[128,512]{1,0:T(8,128)(2,1)S(1)} copy-done((bf16[128,512]{1,0:T(8,128)(2,1)S(1)}, bf16[128,512]{1,0:T(8,128)(2,1)}, u32[]{:S(2)}) %copy-start.5) | copy-done | bytes 131096
  7.4 0.0 copy-start.7
  7.4 0.7 copy-done.7
  8.1 56.9 %shard_map.161 = (bf16[128,512]{1,0:T(8,128)(2,1)S(1)}, bf16[128,512]{1,0:T(8,128)(2,1)S(1)}, bf16[128,512]{1,0:T(8,128)(2,1)S(1)}, bf16[128,512]{1,0:T(8,128)(2...) custom-call(bf16[128,512]{1,0:T(8,128)(2,1)S(1)} %copy-done, ...), custom_call_target="tpu_custom_call" | custom-call | tf_op jit(solution)/shard_map/pallas_call | solution.py:427
  65.0 0.7 copy.27
  65.7 0.7 copy.28
  66.3 0.7 copy.29
  67.0 0.7 copy.30
  67.6 0.7 copy.31
  68.3 0.7 copy.32
  68.9 0.7 copy.33
  69.6 0.7 copy.34
Async XLA Ops:
  0.6 0.7 copy-start.6
  1.3 0.7 copy-start.8
  2.0 0.9 %copy-start = (bf16[128,512]{1,0:T(8,128)(2,1)S(1)}, bf16[128,512]{1,0:T(8,128)(2,1)}, u32[]{:S(2)}) copy-start(bf16[128,512]{1,0:T(8,128)(2,1)} %q_ref.1) | copy-start | bytes 393220
  2.9 0.9 %copy-start.1 = (bf16[128,512]{1,0:T(8,128)(2,1)S(1)}, bf16[128,512]{1,0:T(8,128)(2,1)}, u32[]{:S(2)}) copy-start(bf16[128,512]{1,0:T(8,128)(2,1)} %k_ref.1) | copy-start | bytes 393220
  3.8 0.9 %copy-start.2 = (bf16[128,512]{1,0:T(8,128)(2,1)S(1)}, bf16[128,512]{1,0:T(8,128)(2,1)}, u32[]{:S(2)}) copy-start(bf16[128,512]{1,0:T(8,128)(2,1)} %v_ref.1) | copy-start | bytes 393220
  4.7 0.9 %copy-start.3 = (bf16[128,512]{1,0:T(8,128)(2,1)S(1)}, bf16[128,512]{1,0:T(8,128)(2,1)}, u32[]{:S(2)}) copy-start(bf16[128,512]{1,0:T(8,128)(2,1)} %lk_ref.1) | copy-start | bytes 393220
  5.6 0.9 %copy-start.4 = (bf16[128,512]{1,0:T(8,128)(2,1)S(1)}, bf16[128,512]{1,0:T(8,128)(2,1)}, u32[]{:S(2)}) copy-start(bf16[128,512]{1,0:T(8,128)(2,1)} %lv_ref.1) | copy-start | bytes 393220
  6.5 0.9 %copy-start.5 = (bf16[128,512]{1,0:T(8,128)(2,1)S(1)}, bf16[128,512]{1,0:T(8,128)(2,1)}, u32[]{:S(2)}) copy-start(bf16[128,512]{1,0:T(8,128)(2,1)} %cot_ref.1) | copy-start | bytes 393220
  7.4 0.7 copy-start.7

commit v2 on v1

--- a/solution.py
+++ b/solution.py
@@ -39,9 +39,26 @@
 def kernel(
     n,
     groups,
-    q_ref,
-    k_ref,
-    v_ref,
+    q_hbm,
+    k_hbm,
+    v_hbm,
+    doc_hbm,
+    list_hbm,
+    lk_hbm,
+    lv_hbm,
+    decay_hbm,
+    gain_hbm,
+    cot_hbm,
+    out_hbm,
+    dq_hbm,
+    dk_hbm,
+    dv_hbm,
+    lout_hbm,
+    lqg_hbm,
+    lkg_hbm,
+    lvg_hbm,
+    stage,
+    leaving,
     doc_ref,
     list_ref,
     lk_ref,
@@ -49,14 +66,7 @@
     decay_ref,
     gain_ref,
     cot_ref,
-    out_ref,
-    dq_ref,
-    dk_ref,
-    dv_ref,
-    lout_ref,
-    lqg_ref,
-    lkg_ref,
-    lvg_ref,
+    load,
     kbuf,
     vbuf,
     qbuf,
@@ -84,9 +94,36 @@
     head_send,
     head_recv,
 ):
+    out_ref, dq_ref, dk_ref, dv_ref, lout_ref, lqg_ref, lkg_ref, lvg_ref = [
+        stage.at[i] for i in range(8)
+    ]
+    homes = (out_hbm, dq_hbm, dk_hbm, dv_hbm, lout_hbm, lqg_hbm, lkg_hbm, lvg_hbm)
+    leaves = [
+        pltpu.make_async_copy(stage.at[i], homes[i], leaving.at[i]) for i in range(8)
+    ]
+    q_ref, k_ref, v_ref = qbuf.at[0], kbuf.at[0], vbuf.at[0]
+    loads = [
+        pltpu.make_async_copy(src, dst, load.at[i])
+        for i, (src, dst) in enumerate(
+            [
+                (decay_hbm, decay_ref),
+                (lk_hbm, lk_ref),
+                (lv_hbm, lv_ref),
+                (doc_hbm, doc_ref),
+                (list_hbm, list_ref),
+                (k_hbm, k_ref),
+                (v_hbm, v_ref),
+                (q_hbm, q_ref),
+                (gain_hbm, gain_ref),
+                (cot_hbm, cot_ref),
+            ]
+        )
+    ]
+    for copy in loads:
+        copy.start()
     me = lax.axis_index("ctx")
     group = lax.axis_index("head")
-    heads = q_ref.shape[1] // HD
+    heads = q_hbm.shape[1] // HD
     rows = heads * HD // n
     scaling = 1.0 / math.sqrt(HD)
     cols = [slice(h * HD, (h + 1) * HD) for h in range(heads)]
@@ -167,6 +204,7 @@
             def _():
                 near(kind, d, src, dst, way * d).wait_recv()
 
+    loads[0].wait()
     row_at = lax.broadcasted_iota(jnp.int32, (BLK, BLK), 0)
     col_at = lax.broadcasted_iota(jnp.int32, (BLK, BLK), 1)
     lower = (row_at >= col_at).astype(F32)
@@ -185,6 +223,8 @@
         jnp.where(causal, jnp.exp(jnp.where(causal, at_col[h] - run_row[h : h + 1, :], 0.0)), 0.0)
         for h in range(heads)
     ]
+    loads[1].wait()
+    loads[2].wait()
     updates = [
         tn((lk_ref[:, cols[h]].astype(F32) * leave[h]).astype(BF16), lv_ref[:, cols[h]])
         for h in range(heads)
@@ -202,14 +242,13 @@
             piece = jnp.concatenate([updates[h][j * rows : (j + 1) * rows], tails[h]], axis=0)
             up_send[h * per_head + j] = piece.astype(BF16)
 
-    doc = doc_ref[0].astype(F32)
-    first = list_ref[0, 0].astype(F32)
-    second = list_ref[0, 1].astype(F32)
+    loads[3].wait()
+    loads[4].wait()
+    doc = jnp.full((1, HD), doc_ref[0].astype(F32))
+    first = jnp.broadcast_to(list_ref[:, 0:1].astype(F32), (1, HD))
+    second = jnp.broadcast_to(list_ref[:, 1:2].astype(F32), (1, HD))
     info_at = lax.broadcasted_iota(jnp.int32, (8, HD), 0)
     info[...] = jnp.where(info_at == 0, doc, jnp.where(info_at == 1, first, second))
-    kbuf[0] = k_ref[...]
-    vbuf[0] = v_ref[...]
-    qbuf[0] = q_ref[...]
     for d in range(1, REACH + 1):
 
         @pl.when(me - d < 0)
@@ -225,6 +264,8 @@
             sidebuf[d] = jnp.zeros((8, HD), F32)
             info_right[d] = jnp.full((8, HD), -1.0, F32)
 
+    for copy in loads[5:]:
+        copy.wait()
     pl.semaphore_wait(barrier, n - 1 + groups - 1)
 
     spread(up_send, up_recv, 0)
@@ -250,7 +291,7 @@
     wait_near(1, k_ref, kbuf, 1)
     bias = [jnp.where(causal, 0.0, NEG)]
     for d in range(1, REACH + 1):
-        listed = (jnp.full((1, HD), first) == d - 1.0) | (jnp.full((1, HD), second) == d - 1.0)
+        listed = (first == d - 1.0) | (second == d - 1.0)
         seen = (info_left[d][0:1, :] == doc) & listed
         bias.append(jnp.broadcast_to(jnp.where(seen, 0.0, NEG), (BLK, HD)))
     bias = jnp.concatenate(bias, axis=1)
@@ -272,6 +313,7 @@
         o = nn(weights[h], vbuf[:, :, cols[h]].reshape(-1, HD)).astype(BF16)
         outs.append(o)
         out_ref[:, cols[h]] = o
+    leaves[0].start()
 
     mixing = [
         (nt(outs[h], lk_ref[:, cols[h]]) * damping[h]).astype(BF16) for h in range(heads)
@@ -318,6 +360,11 @@
     inverse = lax.rsqrt(mean)
     factor = jnp.broadcast_to(total[:, HD // 2 : HD // 2 + 1], (BLK, HD)) / (features * mean)
     halves = [((scaled[h] - raws[h] * factor) * inverse).astype(BF16) for h in range(heads)]
+    for h in range(heads):
+        back = tn(qscaled[h], halves[h])
+        for j in range(per_head):
+            back_send[h * per_head + j] = back[j * rows : (j + 1) * rows].astype(BF16)
+    spread(back_send, back_recv, 2)
     mix_grads = []
     deltas = []
     for h in range(heads):
@@ -338,20 +385,18 @@
     sidebuf[0] = side[...]
     send_near(5, gbuf.at[0], gbuf, -1)
     send_near(6, side, sidebuf, -1)
-    for h in range(heads):
-        back = tn(qscaled[h], halves[h])
-        for j in range(per_head):
-            back_send[h * per_head + j] = back[j * rows : (j + 1) * rows].astype(BF16)
-    spread(back_send, back_recv, 2)
-
+
+    leaves[5].start()
     for h in range(heads):
         lout_ref[:, cols[h]] = (raws[h] * inverse * gain_ref[:, cols[h]]).astype(BF16)
+    leaves[4].start()
     for h in range(heads):
         chance = jnp.exp(score[h] - logsum[h])
         cg = nt(gbuf[0, :, cols[h]], vbuf[:, :, cols[h]].reshape(-1, HD))
         sg = (chance * (cg - deltas[h])).astype(BF16)
         keys = kbuf[:, :, cols[h]].reshape(-1, HD)
         dq_ref[:, cols[h]] = (nn(sg, keys) * scaling).astype(BF16)
+    leaves[1].start()
 
     collect(back_send, back_recv, 2)
 
@@ -388,6 +433,8 @@
         cg = nt(v_ref[:, cols[h]], grads)
         sg = (chance * (cg - dels)).astype(BF16)
         dk_ref[:, cols[h]] = (nn(sg, queries) * scaling).astype(BF16)
+    leaves[2].start()
+    leaves[3].start()
 
     collect(later_send, later_recv, 3)
     laters = later_recv[...].astype(F32).reshape(heads * HD, HD).astype(BF16)
@@ -399,6 +446,19 @@
         lvg_ref[:, cols[h]] = (
             value_local[h] + leave[h] * nn(lk_ref[:, cols[h]], later)
         ).astype(BF16)
+    leaves[6].start()
+    leaves[7].start()
+    for copy in leaves:
+        copy.wait()
+
+
+def store_all(*refs):
+    done = refs[16]
+    copies = [pltpu.make_async_copy(refs[i], refs[8 + i], done.at[i]) for i in range(8)]
+    for copy in copies:
+        copy.start()
+    for copy in copies:
+        copy.wait()
 
 
 def body(
@@ -419,17 +479,27 @@
     heads = width // HD
     rows = heads * HD // n
     ext = 16 if rows % 16 == 0 else 8
-    vmem = pl.BlockSpec(memory_space=pltpu.VMEM)
-    smem = pl.BlockSpec(memory_space=pltpu.SMEM)
+    anywhere = pl.BlockSpec(memory_space=pl.ANY)
+    array = pltpu.VMEM((length, width), BF16)
     slots = REACH + 1
     window = pltpu.VMEM((slots, length, width), BF16)
     part = pltpu.VMEM((n, rows, HD), BF16)
-    return pl.pallas_call(
+    results = pl.pallas_call(
         functools.partial(kernel, n, groups),
         out_shape=[jax.ShapeDtypeStruct((length, width), BF16)] * 8,
-        in_specs=[vmem, vmem, vmem, smem, smem, vmem, vmem, vmem, vmem, vmem],
-        out_specs=[vmem] * 8,
+        in_specs=[anywhere] * 10,
+        out_specs=[anywhere] * 8,
         scratch_shapes=[
+            pltpu.VMEM((8, length, width), BF16),
+            pltpu.SemaphoreType.DMA((8,)),
+            pltpu.SMEM((1,), jnp.int32),
+            pltpu.VMEM((1, 2), jnp.int32),
+            array,
+            array,
+            pltpu.VMEM((heads, length), F32),
+            pltpu.VMEM((1, width), F32),
+            array,
+            pltpu.SemaphoreType.DMA((10,)),
             window,
             window,
             window,
@@ -458,7 +528,7 @@
             pltpu.SemaphoreType.DMA((groups,)),
         ],
         compiler_params=pltpu.CompilerParams(
-            collective_id=0, has_side_effects=True, vmem_limit_bytes=32 * 1024 * 1024
+            collective_id=0, has_side_effects=True, vmem_limit_bytes=60 * 1024 * 1024
         ),
     )(
         softmax_query,
@@ -472,6 +542,15 @@
         linear_gain.reshape(1, width),
         linear_cotangent,
     )
+    store = pl.pallas_call(
+        store_all,
+        out_shape=[jax.ShapeDtypeStruct((length, width), BF16)] * 8,
+        in_specs=[anywhere] * 8,
+        out_specs=[anywhere] * 8,
+        scratch_shapes=[pltpu.SemaphoreType.DMA((8,))],
+        compiler_params=pltpu.CompilerParams(vmem_limit_bytes=60 * 1024 * 1024),
+    )
+    return tuple(store(*results))
 
 
 def solution(mesh):

time: 70.5 us -> 88.3 us (1.25)
  Pallas kernels: 56.9 us -> 86.8 us
  local copies, waits for them, and re-layouts: 12 us -> 0 us
    pallas_call x0 -> x1, Pallas kernels: none -> 32.9 us  [body(): return tuple(store(*results))]
    unnamed x26 -> x0, local copies, waits for them, and re-layouts: 12 us -> none
    pallas_call x1, Pallas kernels: 56.9 us -> 53.9 us  [body(): pl.pallas_call(functools.partial(kernel, n, groups), out_shape=[jax.Shape...]
where the time goes in v2:
time: 88.3 us; the launch traced here: 88.1 us
  Pallas kernels  86.8 us (98%)
  between operations  1.29 us (1%)
    pallas_call x1, Pallas kernels, body(): pl.pallas_call(functools.partial(kernel, n, groups), out_shape=[jax.Shape...  53.9 us
    pallas_call x1, Pallas kernels, body(): return tuple(store(*results))  32.9 us

profile of v2, /device:TPU:0, one launch (start us, length us, event | category | flops | bytes accessed | tf_op | source)
XLA Modules:
  0.0 88.1 jit_solution(3524200556453998786)
XLA Ops:
  1.3 53.9 %shard_map.161 = (bf16[128,512]{1,0:T(8,128)(2,1)}, bf16[128,512]{1,0:T(8,128)(2,1)}, bf16[128,512]{1,0:T(8,128)(2,1)}, bf16[128,512]{1,0:T(8,128)(2,1)}, bf16[1...) custom-call(bf16[128,512]{1,0:T(8,128)(2,1)} %q_hbm.1, ...), custom_call_target="tpu_custom_call" | custom-call | tf_op jit(solution)/shard_map/pallas_call | solution.py:487
  55.1 32.9 %shard_map.162 = (bf16[128,512]{1,0:T(8,128)(2,1)}, bf16[128,512]{1,0:T(8,128)(2,1)}, bf16[128,512]{1,0:T(8,128)(2,1)}, bf16[128,512]{1,0:T(8,128)(2,1)}, bf16[1...) custom-call(bf16[128,512]{1,0:T(8,128)(2,1)} %get-tuple-element.16.refs_0_, ...), custom_call_target="tpu_custom_call" | custom-call | tf_op jit(solution)/shard_map/pallas_call | solution.py:553

commit v3 on v2

--- a/solution.py
+++ b/solution.py
@@ -11,6 +11,7 @@
 HD = 128
 BLK = 128
 REACH = 3
+GROUP = 4
 NEG = -1e30
 EPSILON = 1e-05
 MESH = pl.DeviceIdType.MESH
@@ -87,6 +88,9 @@
     later_recv,
     sums,
     sums_recv,
+    relayed,
+    relay_send,
+    relay_recv,
     near_send,
     near_recv,
     far_send,
@@ -183,7 +187,9 @@
             device_id_type=MESH,
         )
 
-    def send_near(kind, src, dst, way):
+    place = lax.rem(me, GROUP)
+
+    def send_small(kind, src, dst, way):
         for d in range(1, REACH + 1):
             target = me + way * d
 
@@ -191,7 +197,7 @@
             def _():
                 near(kind, d, src, dst, way * d).start()
 
-    def wait_near(kind, src, dst, way):
+    def wait_small(kind, src, dst, way):
         for d in range(1, REACH + 1):
             target = me + way * d
             source = me - way * d
@@ -203,6 +209,72 @@
             @pl.when((source >= 0) & (source < n))
             def _():
                 near(kind, d, src, dst, way * d).wait_recv()
+
+    def ahead(way):
+        return place if way > 0 else GROUP - 1 - place
+
+    def inside(way, groups_on):
+        target = me + way * GROUP * groups_on
+        return (ahead(way) >= 1) & (target >= 0) & (target < n)
+
+    def relay(kind, src, way):
+        return pltpu.make_async_remote_copy(
+            src_ref=src,
+            dst_ref=relayed.at[kind],
+            send_sem=relay_send.at[kind],
+            recv_sem=relay_recv.at[kind],
+            device_id={"ctx": lax.rem(me + way * GROUP + n, n)},
+            device_id_type=MESH,
+        )
+
+    def send_across(kind, src, way):
+        @pl.when(inside(way, 1))
+        def _():
+            relay(kind, src, way).start()
+
+    def send_direct(kind, src, dst, way):
+        for d in range(1, REACH + 1):
+
+            @pl.when(ahead(way) + d < GROUP)
+            def _():
+                near(kind, d, src, dst, way * d).start()
+
+    def forward_on(kind, src, dst, way):
+        @pl.when(inside(way, -1))
+        def _():
+            relay(kind, src, way).wait_recv()
+            for e in range(1, GROUP):
+
+                @pl.when(e <= ahead(way))
+                def _():
+                    near(kind, GROUP - e, relayed.at[kind], dst, -way * e).start()
+
+    def wait_block(kind, src, dst, way):
+        for d in range(1, REACH + 1):
+            source = me - way * d
+
+            @pl.when((source >= 0) & (source < n))
+            def _():
+                near(kind, d, src, dst, way * d).wait_recv()
+
+    def wait_sent(kind, src, dst, way):
+        @pl.when(inside(way, 1))
+        def _():
+            relay(kind, src, way).wait_send()
+
+        for d in range(1, REACH + 1):
+
+            @pl.when(ahead(way) + d < GROUP)
+            def _():
+                near(kind, d, src, dst, way * d).wait_send()
+
+        @pl.when(inside(way, -1))
+        def _():
+            for e in range(1, GROUP):
+
+                @pl.when(e <= ahead(way))
+                def _():
+                    near(kind, GROUP - e, relayed.at[kind], dst, -way * e).wait_send()
 
     loads[0].wait()
     row_at = lax.broadcasted_iota(jnp.int32, (BLK, BLK), 0)
@@ -269,10 +341,13 @@
     pl.semaphore_wait(barrier, n - 1 + groups - 1)
 
     spread(up_send, up_recv, 0)
-    send_near(0, info, info_left, 1)
-    send_near(1, k_ref, kbuf, 1)
-    send_near(2, v_ref, vbuf, 1)
-    send_near(3, info, info_right, -1)
+    send_across(1, k_ref, 1)
+    send_small(0, info, info_left, 1)
+    send_direct(1, k_ref, kbuf, 1)
+    send_across(2, v_ref, 1)
+    send_across(4, q_ref, -1)
+    send_direct(2, v_ref, vbuf, 1)
+    send_small(3, info, info_right, -1)
 
     collect(up_send, up_recv, 0)
 
@@ -287,8 +362,10 @@
     lax.fori_loop(0, n, forward, jnp.zeros((rows, HD), F32))
     spread(state_send, state_recv, 1)
 
-    wait_near(0, info, info_left, 1)
-    wait_near(1, k_ref, kbuf, 1)
+    forward_on(1, k_ref, kbuf, 1)
+    forward_on(2, v_ref, vbuf, 1)
+    wait_small(0, info, info_left, 1)
+    wait_block(1, k_ref, kbuf, 1)
     bias = [jnp.where(causal, 0.0, NEG)]
     for d in range(1, REACH + 1):
         listed = (first == d - 1.0) | (second == d - 1.0)
@@ -306,8 +383,9 @@
         total = jnp.sum(e, axis=1, keepdims=True)
         weights.append((e / total).astype(BF16))
         logsum.append(m + jnp.log(total))
-    wait_near(2, v_ref, vbuf, 1)
-    send_near(4, q_ref, qbuf, -1)
+    wait_block(2, v_ref, vbuf, 1)
+    send_direct(4, q_ref, qbuf, -1)
+    forward_on(4, q_ref, qbuf, -1)
     outs = []
     for h in range(heads):
         o = nn(weights[h], vbuf[:, :, cols[h]].reshape(-1, HD)).astype(BF16)
@@ -383,8 +461,9 @@
         block = jnp.where(col_at == heads + h, deltas[h], block)
     side[...] = block.T[0 : 2 * heads, :]
     sidebuf[0] = side[...]
-    send_near(5, gbuf.at[0], gbuf, -1)
-    send_near(6, side, sidebuf, -1)
+    send_across(5, gbuf.at[0], -1)
+    send_direct(5, gbuf.at[0], gbuf, -1)
+    send_small(6, side, sidebuf, -1)
 
     leaves[5].start()
     for h in range(heads):
@@ -397,6 +476,7 @@
         keys = kbuf[:, :, cols[h]].reshape(-1, HD)
         dq_ref[:, cols[h]] = (nn(sg, keys) * scaling).astype(BF16)
     leaves[1].start()
+    forward_on(5, gbuf.at[0], gbuf, -1)
 
     collect(back_send, back_recv, 2)
 
@@ -410,8 +490,8 @@
     key_local = [tn(mix_grads[h], outs[h]) for h in range(heads)]
     value_local = [tn(mixing[h], halves[h]) for h in range(heads)]
 
-    wait_near(3, info, info_right, -1)
-    wait_near(4, q_ref, qbuf, -1)
+    wait_small(3, info, info_right, -1)
+    wait_block(4, q_ref, qbuf, -1)
     bias = [jnp.where(row_at <= col_at, 0.0, NEG)]
     for d in range(1, REACH + 1):
         theirs = info_right[d]
@@ -419,8 +499,8 @@
         seen = (theirs[0:1, :] == doc) & listed
         bias.append(jnp.broadcast_to(jnp.where(seen, 0.0, NEG), (BLK, HD)))
     bias = jnp.concatenate(bias, axis=1)
-    wait_near(5, gbuf.at[0], gbuf, -1)
-    wait_near(6, side, sidebuf, -1)
+    wait_block(5, gbuf.at[0], gbuf, -1)
+    wait_small(6, side, sidebuf, -1)
     for h in range(heads):
         queries = qbuf[:, :, cols[h]].reshape(-1, HD)
         grads = gbuf[:, :, cols[h]].reshape(-1, HD)
@@ -448,17 +528,25 @@
         ).astype(BF16)
     leaves[6].start()
     leaves[7].start()
+    wait_sent(1, k_ref, kbuf, 1)
+    wait_sent(2, v_ref, vbuf, 1)
+    wait_sent(4, q_ref, qbuf, -1)
+    wait_sent(5, gbuf.at[0], gbuf, -1)
     for copy in leaves:
         copy.wait()
 
 
 def store_all(*refs):
-    done = refs[16]
-    copies = [pltpu.make_async_copy(refs[i], refs[8 + i], done.at[i]) for i in range(8)]
-    for copy in copies:
-        copy.start()
-    for copy in copies:
-        copy.wait()
+    held, arrived, done = refs[16:]
+    loads = [pltpu.make_async_copy(refs[i], held.at[i], arrived.at[i]) for i in range(8)]
+    stores = [pltpu.make_async_copy(held.at[i], refs[8 + i], done.at[i]) for i in range(8)]
+    for load in loads:
+        load.start()
+    for load, store in zip(loads, stores):
+        load.wait()
+        store.start()
+    for store in stores:
+        store.wait()
 
 
 def body(
@@ -520,6 +608,9 @@
             part,
             pltpu.VMEM((length, HD), F32),
             pltpu.VMEM((groups, length, HD), F32),
+            pltpu.VMEM((6, length, width), BF16),
+            pltpu.SemaphoreType.DMA((6,)),
+            pltpu.SemaphoreType.DMA((6,)),
             pltpu.SemaphoreType.DMA((7, slots)),
             pltpu.SemaphoreType.DMA((7, slots)),
             pltpu.SemaphoreType.DMA((4, n)),
@@ -547,7 +638,11 @@
         out_shape=[jax.ShapeDtypeStruct((length, width), BF16)] * 8,
         in_specs=[anywhere] * 8,
         out_specs=[anywhere] * 8,
-        scratch_shapes=[pltpu.SemaphoreType.DMA((8,))],
+        scratch_shapes=[
+            pltpu.VMEM((8, length, width), BF16),
+            pltpu.SemaphoreType.DMA((8,)),
+            pltpu.SemaphoreType.DMA((8,)),
+        ],
         compiler_params=pltpu.CompilerParams(vmem_limit_bytes=60 * 1024 * 1024),
     )
     return tuple(store(*results))

time: 88.3 us -> 56.5 us (0.64)
  the two profiles are of different devices: /device:TPU:0 before, /device:TPU:14 now
where the time goes in v3:
time: 56.5 us; the launch traced here: 56.4 us
  Pallas kernels  55.1 us (98%)
  between operations  1.29 us (2%)
    pallas_call x1, Pallas kernels, body(): pl.pallas_call(functools.partial(kernel, n, groups), out_shape=[jax.Shape...  53 us
    pallas_call x1, Pallas kernels, body(): return tuple(store(*results))  2.09 us

profile of v3, /device:TPU:14, one launch (start us, length us, event | category | flops | bytes accessed | tf_op | source)
XLA Modules:
  0.0 56.4 jit_solution(2100032769402476642)
XLA Ops:
  1.3 53.0 %shard_map.161 = (bf16[128,512]{1,0:T(8,128)(2,1)}, bf16[128,512]{1,0:T(8,128)(2,1)}, bf16[128,512]{1,0:T(8,128)(2,1)}, bf16[128,512]{1,0:T(8,128)(2,1)}, bf16[1...) custom-call(bf16[128,512]{1,0:T(8,128)(2,1)} %q_hbm.1, ...), custom_call_target="tpu_custom_call" | custom-call | tf_op jit(solution)/shard_map/pallas_call | solution.py:575
  54.3 2.1 %shard_map.162 = (bf16[128,512]{1,0:T(8,128)(2,1)}, bf16[128,512]{1,0:T(8,128)(2,1)}, bf16[128,512]{1,0:T(8,128)(2,1)}, bf16[128,512]{1,0:T(8,128)(2,1)}, bf16[1...) custom-call(bf16[128,512]{1,0:T(8,128)(2,1)} %get-tuple-element.16.refs_0_, ...), custom_call_target="tpu_custom_call" | custom-call | tf_op jit(solution)/shard_map/pallas_call | solution.py:648

commit v4 on v3

--- a/solution.py
+++ b/solution.py
@@ -77,6 +77,8 @@
     info_right,
     side,
     sidebuf,
+    logs_out,
+    logsbuf,
     score,
     up_send,
     up_recv,
@@ -110,14 +112,14 @@
         pltpu.make_async_copy(src, dst, load.at[i])
         for i, (src, dst) in enumerate(
             [
+                (k_hbm, k_ref),
+                (v_hbm, v_ref),
+                (q_hbm, q_ref),
                 (decay_hbm, decay_ref),
                 (lk_hbm, lk_ref),
                 (lv_hbm, lv_ref),
                 (doc_hbm, doc_ref),
                 (list_hbm, list_ref),
-                (k_hbm, k_ref),
-                (v_hbm, v_ref),
-                (q_hbm, q_ref),
                 (gain_hbm, gain_ref),
                 (cot_hbm, cot_ref),
             ]
@@ -277,6 +279,16 @@
                     near(kind, GROUP - e, relayed.at[kind], dst, -way * e).wait_send()
 
     loads[0].wait()
+    loads[1].wait()
+    pl.semaphore_wait(barrier, n - 1 + groups - 1)
+    send_across(1, k_ref, 1)
+    send_direct(1, k_ref, kbuf, 1)
+    send_across(2, v_ref, 1)
+    send_direct(2, v_ref, vbuf, 1)
+    loads[2].wait()
+    send_across(4, q_ref, -1)
+
+    loads[3].wait()
     row_at = lax.broadcasted_iota(jnp.int32, (BLK, BLK), 0)
     col_at = lax.broadcasted_iota(jnp.int32, (BLK, BLK), 1)
     lower = (row_at >= col_at).astype(F32)
@@ -295,8 +307,8 @@
         jnp.where(causal, jnp.exp(jnp.where(causal, at_col[h] - run_row[h : h + 1, :], 0.0)), 0.0)
         for h in range(heads)
     ]
-    loads[1].wait()
-    loads[2].wait()
+    loads[4].wait()
+    loads[5].wait()
     updates = [
         tn((lk_ref[:, cols[h]].astype(F32) * leave[h]).astype(BF16), lv_ref[:, cols[h]])
         for h in range(heads)
@@ -314,8 +326,8 @@
             piece = jnp.concatenate([updates[h][j * rows : (j + 1) * rows], tails[h]], axis=0)
             up_send[h * per_head + j] = piece.astype(BF16)
 
-    loads[3].wait()
-    loads[4].wait()
+    loads[6].wait()
+    loads[7].wait()
     doc = jnp.full((1, HD), doc_ref[0].astype(F32))
     first = jnp.broadcast_to(list_ref[:, 0:1].astype(F32), (1, HD))
     second = jnp.broadcast_to(list_ref[:, 1:2].astype(F32), (1, HD))
@@ -333,21 +345,15 @@
         def _():
             qbuf[d] = jnp.zeros_like(qbuf[d])
             gbuf[d] = jnp.zeros_like(gbuf[d])
-            sidebuf[d] = jnp.zeros((8, HD), F32)
+            sidebuf[d] = jnp.zeros((2 * heads, HD), F32)
+            logsbuf[d] = jnp.zeros((2 * heads, HD), F32)
             info_right[d] = jnp.full((8, HD), -1.0, F32)
 
-    for copy in loads[5:]:
-        copy.wait()
-    pl.semaphore_wait(barrier, n - 1 + groups - 1)
-
+    send_small(0, info, info_left, 1)
+    send_small(3, info, info_right, -1)
+    forward_on(1, k_ref, kbuf, 1)
     spread(up_send, up_recv, 0)
-    send_across(1, k_ref, 1)
-    send_small(0, info, info_left, 1)
-    send_direct(1, k_ref, kbuf, 1)
-    send_across(2, v_ref, 1)
-    send_across(4, q_ref, -1)
-    send_direct(2, v_ref, vbuf, 1)
-    send_small(3, info, info_right, -1)
+    forward_on(2, v_ref, vbuf, 1)
 
     collect(up_send, up_recv, 0)
 
@@ -362,8 +368,6 @@
     lax.fori_loop(0, n, forward, jnp.zeros((rows, HD), F32))
     spread(state_send, state_recv, 1)
 
-    forward_on(1, k_ref, kbuf, 1)
-    forward_on(2, v_ref, vbuf, 1)
     wait_small(0, info, info_left, 1)
     wait_block(1, k_ref, kbuf, 1)
     bias = [jnp.where(causal, 0.0, NEG)]
@@ -381,11 +385,19 @@
         m = jnp.max(s, axis=1, keepdims=True)
         e = jnp.exp(s - m)
         total = jnp.sum(e, axis=1, keepdims=True)
-        weights.append((e / total).astype(BF16))
+        weights.append((e * (1.0 / total)).astype(BF16))
         logsum.append(m + jnp.log(total))
+    block = jnp.zeros((BLK, HD), F32)
+    for h in range(heads):
+        block = jnp.where(col_at == h, logsum[h], block)
+    logs_out[...] = block.T[0 : 2 * heads, :]
+    logsbuf[0] = logs_out[...]
+    send_small(7, logs_out, logsbuf, -1)
     wait_block(2, v_ref, vbuf, 1)
     send_direct(4, q_ref, qbuf, -1)
     forward_on(4, q_ref, qbuf, -1)
+    loads[8].wait()
+    loads[9].wait()
     outs = []
     for h in range(heads):
         o = nn(weights[h], vbuf[:, :, cols[h]].reshape(-1, HD)).astype(BF16)
@@ -438,13 +450,9 @@
     inverse = lax.rsqrt(mean)
     factor = jnp.broadcast_to(total[:, HD // 2 : HD // 2 + 1], (BLK, HD)) / (features * mean)
     halves = [((scaled[h] - raws[h] * factor) * inverse).astype(BF16) for h in range(heads)]
-    for h in range(heads):
-        back = tn(qscaled[h], halves[h])
-        for j in range(per_head):
-            back_send[h * per_head + j] = back[j * rows : (j + 1) * rows].astype(BF16)
-    spread(back_send, back_recv, 2)
     mix_grads = []
     deltas = []
+    gs = []
     for h in range(heads):
         mg = (nt(halves[h], lv_ref[:, cols[h]]) * damping[h]).astype(BF16)
         mix_grads.append(mg)
@@ -452,18 +460,25 @@
         g = g.astype(BF16)
         lqg_ref[:, cols[h]] = g
         gbuf[0, :, cols[h]] = g
+        gs.append(g)
+    send_across(5, gbuf.at[0], -1)
+    send_direct(5, gbuf.at[0], gbuf, -1)
+    for h in range(heads):
+        g = gs[h]
         deltas.append(
             jnp.sum(g.astype(F32) * outs[h].astype(F32), axis=1, keepdims=True)
         )
     block = jnp.zeros((BLK, HD), F32)
     for h in range(heads):
-        block = jnp.where(col_at == h, logsum[h], block)
-        block = jnp.where(col_at == heads + h, deltas[h], block)
+        block = jnp.where(col_at == h, deltas[h], block)
     side[...] = block.T[0 : 2 * heads, :]
     sidebuf[0] = side[...]
-    send_across(5, gbuf.at[0], -1)
-    send_direct(5, gbuf.at[0], gbuf, -1)
     send_small(6, side, sidebuf, -1)
+    for h in range(heads):
+        back = tn(qscaled[h], halves[h])
+        for j in range(per_head):
+            back_send[h * per_head + j] = back[j * rows : (j + 1) * rows].astype(BF16)
+    spread(back_send, back_recv, 2)
 
     leaves[5].start()
     for h in range(heads):
@@ -499,16 +514,20 @@
         seen = (theirs[0:1, :] == doc) & listed
         bias.append(jnp.broadcast_to(jnp.where(seen, 0.0, NEG), (BLK, HD)))
     bias = jnp.concatenate(bias, axis=1)
+    wait_small(7, logs_out, logsbuf, -1)
+    for h in range(heads):
+        queries = qbuf[:, :, cols[h]].reshape(-1, HD)
+        logs = jnp.concatenate([logsbuf[d, h : h + 1, :] for d in range(REACH + 1)], axis=1)
+        score[h] = jnp.exp(nt(k_ref[:, cols[h]], queries) * scaling + bias - logs)
     wait_block(5, gbuf.at[0], gbuf, -1)
     wait_small(6, side, sidebuf, -1)
     for h in range(heads):
         queries = qbuf[:, :, cols[h]].reshape(-1, HD)
         grads = gbuf[:, :, cols[h]].reshape(-1, HD)
-        logs = jnp.concatenate([sidebuf[d, h : h + 1, :] for d in range(REACH + 1)], axis=1)
         dels = jnp.concatenate(
-            [sidebuf[d, heads + h : heads + h + 1, :] for d in range(REACH + 1)], axis=1
-        )
-        chance = jnp.exp(nt(k_ref[:, cols[h]], queries) * scaling + bias - logs)
+            [sidebuf[d, h : h + 1, :] for d in range(REACH + 1)], axis=1
+        )
+        chance = score[h]
         dv_ref[:, cols[h]] = nn(chance.astype(BF16), grads).astype(BF16)
         cg = nt(v_ref[:, cols[h]], grads)
         sg = (chance * (cg - dels)).astype(BF16)
@@ -597,6 +616,8 @@
             pltpu.VMEM((slots, 8, HD), F32),
             pltpu.VMEM((2 * heads, HD), F32),
             pltpu.VMEM((slots, 2 * heads, HD), F32),
+            pltpu.VMEM((2 * heads, HD), F32),
+            pltpu.VMEM((slots, 2 * heads, HD), F32),
             pltpu.VMEM((heads, length, slots * HD), F32),
             pltpu.VMEM((n, rows + ext, HD), BF16),
             pltpu.VMEM((n, rows + ext, HD), BF16),
@@ -611,8 +632,8 @@
             pltpu.VMEM((6, length, width), BF16),
             pltpu.SemaphoreType.DMA((6,)),
             pltpu.SemaphoreType.DMA((6,)),
-            pltpu.SemaphoreType.DMA((7, slots)),
-            pltpu.SemaphoreType.DMA((7, slots)),
+            pltpu.SemaphoreType.DMA((8, slots)),
+            pltpu.SemaphoreType.DMA((8, slots)),
             pltpu.SemaphoreType.DMA((4, n)),
             pltpu.SemaphoreType.DMA((4, n)),
             pltpu.SemaphoreType.DMA((groups,)),

time: 56.5 us -> 51.7 us (0.915)
  the two profiles are of different devices: /device:TPU:14 before, /device:TPU:0 now
where the time goes in v4:
time: 51.7 us; the launch traced here: 51.4 us
  Pallas kernels  50.1 us (97%)
  between operations  1.29 us (2%)
    pallas_call x1, Pallas kernels, body(): pl.pallas_call(functools.partial(kernel, n, groups), out_shape=[jax.Shape...  48.1 us
    pallas_call x1, Pallas kernels, body(): return tuple(store(*results))  2.09 us

profile of v4, /device:TPU:0, one launch (start us, length us, event | category | flops | bytes accessed | tf_op | source)
XLA Modules:
  0.0 51.4 jit_solution(18238144063706984906)
XLA Ops:
  1.3 48.1 %shard_map.161 = (bf16[128,512]{1,0:T(8,128)(2,1)}, bf16[128,512]{1,0:T(8,128)(2,1)}, bf16[128,512]{1,0:T(8,128)(2,1)}, bf16[128,512]{1,0:T(8,128)(2,1)}, bf16[1...) custom-call(bf16[128,512]{1,0:T(8,128)(2,1)} %q_hbm.1, ...), custom_call_target="tpu_custom_call" | custom-call | tf_op jit(solution)/shard_map/pallas_call | solution.py:594
  49.3 2.1 %shard_map.162 = (bf16[128,512]{1,0:T(8,128)(2,1)}, bf16[128,512]{1,0:T(8,128)(2,1)}, bf16[128,512]{1,0:T(8,128)(2,1)}, bf16[128,512]{1,0:T(8,128)(2,1)}, bf16[1...) custom-call(bf16[128,512]{1,0:T(8,128)(2,1)} %get-tuple-element.16.refs_0_, ...), custom_call_target="tpu_custom_call" | custom-call | tf_op jit(solution)/shard_map/pallas_call | solution.py:669

commit v5 on v4

--- a/solution.py
+++ b/solution.py
@@ -12,6 +12,7 @@
 BLK = 128
 REACH = 3
 GROUP = 4
+TAIL = 16
 NEG = -1e30
 EPSILON = 1e-05
 MESH = pl.DeviceIdType.MESH
@@ -95,8 +96,12 @@
     relay_recv,
     near_send,
     near_recv,
-    far_send,
-    far_recv,
+    total_send,
+    total_recv,
+    total_sent,
+    total_got,
+    plane_send,
+    plane_recv,
     head_send,
     head_recv,
 ):
@@ -130,9 +135,10 @@
     me = lax.axis_index("ctx")
     group = lax.axis_index("head")
     heads = q_hbm.shape[1] // HD
-    rows = heads * HD // n
     scaling = 1.0 / math.sqrt(HD)
     cols = [slice(h * HD, (h + 1) * HD) for h in range(heads)]
+
+    ext_at = lax.broadcasted_iota(jnp.int32, (TAIL, HD), 0)
 
     barrier = pltpu.get_barrier_semaphore()
 
@@ -148,36 +154,91 @@
             barrier, inc=1, device_id={"head": lax.rem(group + o, groups)}, device_id_type=MESH
         )
 
-    def spread(src, dst, lane):
-        def one(o, c):
-            j = lax.rem(me + o, n)
+    place = lax.rem(me, GROUP)
+    plane = me // GROUP
+    planes = n // GROUP
+
+    def spread(lane, src, dst):
+        for o in range(1, GROUP):
+            j = lax.rem(place + o, GROUP)
             pltpu.make_async_remote_copy(
                 src_ref=src.at[j],
-                dst_ref=dst.at[me],
-                send_sem=far_send.at[lane, j],
-                recv_sem=far_recv.at[lane, me],
-                device_id={"ctx": j},
+                dst_ref=dst.at[place],
+                send_sem=plane_send.at[lane, j],
+                recv_sem=plane_recv.at[lane, place],
+                device_id={"ctx": me - place + j},
                 device_id_type=MESH,
             ).start()
-            return c
-
-        lax.fori_loop(1, n, one, 0)
-        dst[me] = src[me]
-
-    def collect(src, dst, lane):
-        def one(o, c):
-            j = lax.rem(me + n - o, n)
+        dst[place] = src[place]
+
+    def collect(lane, src, dst):
+        for o in range(1, GROUP):
+            j = lax.rem(place + GROUP - o, GROUP)
             pltpu.make_async_remote_copy(
                 src_ref=src.at[j],
                 dst_ref=dst.at[j],
-                send_sem=far_send.at[lane, j],
-                recv_sem=far_recv.at[lane, j],
-                device_id={"ctx": j},
+                send_sem=plane_send.at[lane, j],
+                recv_sem=plane_recv.at[lane, j],
+                device_id={"ctx": me - place + j},
                 device_id_type=MESH,
             ).wait()
-            return c
-
-        lax.fori_loop(1, n, one, 0)
+
+    def total_to(lane, o, way):
+        return pltpu.make_async_remote_copy(
+            src_ref=total_send.at[lane],
+            dst_ref=total_recv.at[lane, o],
+            send_sem=total_sent.at[lane, o],
+            recv_sem=total_got.at[lane, o],
+            device_id={"ctx": lax.rem(me + way * GROUP * o + n, n)},
+            device_id_type=MESH,
+        )
+
+    def within(target):
+        return (target >= 0) & (target < planes)
+
+    def send_totals(lane, way):
+        for o in range(1, planes):
+
+            @pl.when(within(plane + way * o))
+            def _():
+                total_to(lane, o, way).start()
+
+    def wait_totals(lane, way):
+        for o in range(1, planes):
+
+            @pl.when(within(plane + way * o))
+            def _():
+                total_to(lane, o, way).wait_send()
+
+            @pl.when(within(plane - way * o))
+            def _():
+                total_to(lane, o, way).wait_recv()
+
+    def with_tail(value, factor):
+        high = factor.astype(BF16).astype(F32)
+        tail = jnp.where(ext_at < TAIL // 2, high, factor - high)
+        return jnp.concatenate([value, tail], axis=0).astype(BF16)
+
+    def tail_of(piece):
+        tail = piece[HD:, :].astype(F32)
+        return tail[0:1, :] + tail[TAIL // 2 : TAIL // 2 + 1, :]
+
+    def scan_plane(terms, factors, order):
+        state = jnp.zeros((HD, HD), F32)
+        product = jnp.ones((1, HD), F32)
+        starts = [None] * GROUP
+        for p in order:
+            starts[p] = (state, product)
+            state = factors[p] * state + terms[p]
+            product = factors[p] * product
+        return starts, state, product
+
+    def incoming(lane, count):
+        def one(i, state):
+            piece = total_recv[lane, count - i]
+            return tail_of(piece) * state + piece[:HD, :].astype(F32)
+
+        return lax.fori_loop(0, count, one, jnp.zeros((HD, HD), F32))
 
     def near(kind, d, src, dst, step):
         return pltpu.make_async_remote_copy(
@@ -188,8 +249,6 @@
             device_id={"ctx": lax.rem(me + step + n, n)},
             device_id_type=MESH,
         )
-
-    place = lax.rem(me, GROUP)
 
     def send_small(kind, src, dst, way):
         for d in range(1, REACH + 1):
@@ -313,19 +372,8 @@
         tn((lk_ref[:, cols[h]].astype(F32) * leave[h]).astype(BF16), lv_ref[:, cols[h]])
         for h in range(heads)
     ]
-    ext = up_send.shape[1] - rows
-    high = carry.astype(BF16).astype(F32)
-    low = carry - high
-    ext_at = lax.broadcasted_iota(jnp.int32, (ext, HD), 0)
-    tails = [
-        jnp.where(ext_at < ext // 2, high[h : h + 1, :], low[h : h + 1, :]) for h in range(heads)
-    ]
-    per_head = n // heads
-    for h in range(heads):
-        for j in range(per_head):
-            piece = jnp.concatenate([updates[h][j * rows : (j + 1) * rows], tails[h]], axis=0)
-            up_send[h * per_head + j] = piece.astype(BF16)
-
+    for h in range(heads):
+        up_send[h] = with_tail(updates[h], carry[h : h + 1, :])
     loads[6].wait()
     loads[7].wait()
     doc = jnp.full((1, HD), doc_ref[0].astype(F32))
@@ -351,22 +399,22 @@
 
     send_small(0, info, info_left, 1)
     send_small(3, info, info_right, -1)
+    spread(0, up_send, up_recv)
     forward_on(1, k_ref, kbuf, 1)
-    spread(up_send, up_recv, 0)
+
+    collect(0, up_send, up_recv)
+    pieces = [up_recv[p] for p in range(GROUP)]
+    factors = [tail_of(piece) for piece in pieces]
+    terms = [piece[:HD, :].astype(F32) for piece in pieces]
+    starts, state, product = scan_plane(terms, factors, range(GROUP))
+    total_send[0] = with_tail(state, product)
+    send_totals(0, 1)
     forward_on(2, v_ref, vbuf, 1)
-
-    collect(up_send, up_recv, 0)
-
-    def carry_of(p):
-        tail = up_recv[p, rows:, :].astype(F32)
-        return tail[0:1, :] + tail[ext // 2 : ext // 2 + 1, :]
-
-    def forward(p, state):
-        state_send[p] = state.astype(BF16)
-        return carry_of(p) * state + up_recv[p, :rows, :].astype(F32)
-
-    lax.fori_loop(0, n, forward, jnp.zeros((rows, HD), F32))
-    spread(state_send, state_recv, 1)
+    wait_totals(0, 1)
+    state = incoming(0, plane)
+    for p in range(GROUP):
+        state_send[p] = (starts[p][1] * state + starts[p][0]).astype(BF16)
+    spread(1, state_send, state_recv)
 
     wait_small(0, info, info_left, 1)
     wait_block(1, k_ref, kbuf, 1)
@@ -409,8 +457,8 @@
         (nt(outs[h], lk_ref[:, cols[h]]) * damping[h]).astype(BF16) for h in range(heads)
     ]
     inner = [nn(mixing[h], lv_ref[:, cols[h]]) for h in range(heads)]
-    collect(state_send, state_recv, 1)
-    states = state_recv[...].astype(F32).reshape(heads * HD, HD).astype(BF16)
+    collect(1, state_send, state_recv)
+    states = state_recv[...].reshape(heads * HD, HD)
     raws = []
     scaled = []
     squares = jnp.zeros((BLK, HD), F32)
@@ -476,9 +524,8 @@
     send_small(6, side, sidebuf, -1)
     for h in range(heads):
         back = tn(qscaled[h], halves[h])
-        for j in range(per_head):
-            back_send[h * per_head + j] = back[j * rows : (j + 1) * rows].astype(BF16)
-    spread(back_send, back_recv, 2)
+        back_send[h] = back.astype(BF16)
+    spread(2, back_send, back_recv)
 
     leaves[5].start()
     for h in range(heads):
@@ -491,19 +538,21 @@
         keys = kbuf[:, :, cols[h]].reshape(-1, HD)
         dq_ref[:, cols[h]] = (nn(sg, keys) * scaling).astype(BF16)
     leaves[1].start()
-    forward_on(5, gbuf.at[0], gbuf, -1)
-
-    collect(back_send, back_recv, 2)
-
-    def backward(i, state):
-        p = n - 1 - i
-        later_send[p] = state.astype(BF16)
-        return carry_of(p) * state + back_recv[p].astype(F32)
-
-    lax.fori_loop(0, n, backward, jnp.zeros((rows, HD), F32))
-    spread(later_send, later_recv, 3)
+
+    collect(2, back_send, back_recv)
+    terms = [back_recv[p].astype(F32) for p in range(GROUP)]
+    factors = [tail_of(up_recv[p]) for p in range(GROUP)]
+    starts, state, product = scan_plane(terms, factors, range(GROUP - 1, -1, -1))
+    total_send[1] = with_tail(state, product)
+    send_totals(1, -1)
     key_local = [tn(mix_grads[h], outs[h]) for h in range(heads)]
     value_local = [tn(mixing[h], halves[h]) for h in range(heads)]
+    forward_on(5, gbuf.at[0], gbuf, -1)
+    wait_totals(1, -1)
+    state = incoming(1, planes - 1 - plane)
+    for p in range(GROUP):
+        later_send[p] = (starts[p][1] * state + starts[p][0]).astype(BF16)
+    spread(3, later_send, later_recv)
 
     wait_small(3, info, info_right, -1)
     wait_block(4, q_ref, qbuf, -1)
@@ -535,8 +584,8 @@
     leaves[2].start()
     leaves[3].start()
 
-    collect(later_send, later_recv, 3)
-    laters = later_recv[...].astype(F32).reshape(heads * HD, HD).astype(BF16)
+    collect(3, later_send, later_recv)
+    laters = later_recv[...].reshape(heads * HD, HD)
     for h in range(heads):
         later = laters[h * HD : (h + 1) * HD]
         lkg_ref[:, cols[h]] = (
@@ -584,13 +633,12 @@
     groups = lax.axis_size("head")
     length, width = softmax_query.shape
     heads = width // HD
-    rows = heads * HD // n
-    ext = 16 if rows % 16 == 0 else 8
+    assert heads == GROUP and n % GROUP == 0
     anywhere = pl.BlockSpec(memory_space=pl.ANY)
     array = pltpu.VMEM((length, width), BF16)
     slots = REACH + 1
     window = pltpu.VMEM((slots, length, width), BF16)
-    part = pltpu.VMEM((n, rows, HD), BF16)
+    part = pltpu.VMEM((GROUP, HD, HD), BF16)
     results = pl.pallas_call(
         functools.partial(kernel, n, groups),
         out_shape=[jax.ShapeDtypeStruct((length, width), BF16)] * 8,
@@ -619,8 +667,8 @@
             pltpu.VMEM((2 * heads, HD), F32),
             pltpu.VMEM((slots, 2 * heads, HD), F32),
             pltpu.VMEM((heads, length, slots * HD), F32),
-            pltpu.VMEM((n, rows + ext, HD), BF16),
-            pltpu.VMEM((n, rows + ext, HD), BF16),
+            pltpu.VMEM((GROUP, HD + TAIL, HD), BF16),
+            pltpu.VMEM((GROUP, HD + TAIL, HD), BF16),
             part,
             part,
             part,
@@ -634,8 +682,12 @@
             pltpu.SemaphoreType.DMA((6,)),
             pltpu.SemaphoreType.DMA((8, slots)),
             pltpu.SemaphoreType.DMA((8, slots)),
-            pltpu.SemaphoreType.DMA((4, n)),
-            pltpu.SemaphoreType.DMA((4, n)),
+            pltpu.VMEM((2, HD + TAIL, HD), BF16),
+            pltpu.VMEM((2, n // GROUP, HD + TAIL, HD), BF16),
+            pltpu.SemaphoreType.DMA((2, n // GROUP)),
+            pltpu.SemaphoreType.DMA((2, n // GROUP)),
+            pltpu.SemaphoreType.DMA((4, GROUP)),
+            pltpu.SemaphoreType.DMA((4, GROUP)),
             pltpu.SemaphoreType.DMA((groups,)),
             pltpu.SemaphoreType.DMA((groups,)),
         ],

time: 51.7 us -> 56.9 us (1.10)
  Pallas kernels: 50.1 us -> 55.5 us
    pallas_call x1, Pallas kernels: 48.1 us -> 53.4 us  [body(): pl.pallas_call(functools.partial(kernel, n, groups), out_shape=[jax.Shape...]
where the time goes in v5:
time: 56.9 us; the launch traced here: 56.8 us
  Pallas kernels  55.5 us (98%)
  between operations  1.29 us (2%)
    pallas_call x1, Pallas kernels, body(): pl.pallas_call(functools.partial(kernel, n, groups), out_shape=[jax.Shape...  53.4 us
    pallas_call x1, Pallas kernels, body(): return tuple(store(*results))  2.09 us

profile of v5, /device:TPU:0, one launch (start us, length us, event | category | flops | bytes accessed | tf_op | source)
XLA Modules:
  0.0 56.8 jit_solution(1433793080805487230)
XLA Ops:
  1.3 53.4 %shard_map.161 = (bf16[128,512]{1,0:T(8,128)(2,1)}, bf16[128,512]{1,0:T(8,128)(2,1)}, bf16[128,512]{1,0:T(8,128)(2,1)}, bf16[128,512]{1,0:T(8,128)(2,1)}, bf16[1...) custom-call(bf16[128,512]{1,0:T(8,128)(2,1)} %q_hbm.1, ...), custom_call_target="tpu_custom_call" | custom-call | tf_op jit(solution)/shard_map/pallas_call | solution.py:642
  54.7 2.1 %shard_map.162 = (bf16[128,512]{1,0:T(8,128)(2,1)}, bf16[128,512]{1,0:T(8,128)(2,1)}, bf16[128,512]{1,0:T(8,128)(2,1)}, bf16[128,512]{1,0:T(8,128)(2,1)}, bf16[1...) custom-call(bf16[128,512]{1,0:T(8,128)(2,1)} %get-tuple-element.16.refs_0_, ...), custom_call_target="tpu_custom_call" | custom-call | tf_op jit(solution)/shard_map/pallas_call | solution.py:721

commit v6 on v5

--- a/solution.py
+++ b/solution.py
@@ -337,16 +337,6 @@
                 def _():
                     near(kind, GROUP - e, relayed.at[kind], dst, -way * e).wait_send()
 
-    loads[0].wait()
-    loads[1].wait()
-    pl.semaphore_wait(barrier, n - 1 + groups - 1)
-    send_across(1, k_ref, 1)
-    send_direct(1, k_ref, kbuf, 1)
-    send_across(2, v_ref, 1)
-    send_direct(2, v_ref, vbuf, 1)
-    loads[2].wait()
-    send_across(4, q_ref, -1)
-
     loads[3].wait()
     row_at = lax.broadcasted_iota(jnp.int32, (BLK, BLK), 0)
     col_at = lax.broadcasted_iota(jnp.int32, (BLK, BLK), 1)
@@ -354,18 +344,12 @@
     rates = decay_ref[...]
     exact = lax.Precision.HIGHEST
     run_col = dot(lower, rates, ((1,), (1,)), exact)
-    run_row = dot(rates, lower, ((1,), (1,)), exact)
     last = dot(rates, jnp.ones((BLK, BLK), F32), ((1,), (0,)), exact)
     carry = jnp.exp(last)
     causal = row_at >= col_at
 
     at_col = [jnp.broadcast_to(run_col[:, h : h + 1], (BLK, HD)) for h in range(heads)]
     leave = [jnp.exp(last[h : h + 1, :] - at_col[h]) for h in range(heads)]
-    enter = [jnp.exp(at_col[h]) for h in range(heads)]
-    damping = [
-        jnp.where(causal, jnp.exp(jnp.where(causal, at_col[h] - run_row[h : h + 1, :], 0.0)), 0.0)
-        for h in range(heads)
-    ]
     loads[4].wait()
     loads[5].wait()
     updates = [
@@ -381,6 +365,23 @@
     second = jnp.broadcast_to(list_ref[:, 1:2].astype(F32), (1, HD))
     info_at = lax.broadcasted_iota(jnp.int32, (8, HD), 0)
     info[...] = jnp.where(info_at == 0, doc, jnp.where(info_at == 1, first, second))
+    pl.semaphore_wait(barrier, n - 1 + groups - 1)
+    spread(0, up_send, up_recv)
+    send_small(0, info, info_left, 1)
+    loads[0].wait()
+    loads[1].wait()
+    send_across(1, k_ref, 1)
+    send_direct(1, k_ref, kbuf, 1)
+    send_across(2, v_ref, 1)
+    send_direct(2, v_ref, vbuf, 1)
+    loads[2].wait()
+    send_across(4, q_ref, -1)
+    run_row = dot(rates, lower, ((1,), (1,)), exact)
+    enter = [jnp.exp(at_col[h]) for h in range(heads)]
+    damping = [
+        jnp.where(causal, jnp.exp(jnp.where(causal, at_col[h] - run_row[h : h + 1, :], 0.0)), 0.0)
+        for h in range(heads)
+    ]
     for d in range(1, REACH + 1):
 
         @pl.when(me - d < 0)
@@ -397,9 +398,7 @@
             logsbuf[d] = jnp.zeros((2 * heads, HD), F32)
             info_right[d] = jnp.full((8, HD), -1.0, F32)
 
-    send_small(0, info, info_left, 1)
     send_small(3, info, info_right, -1)
-    spread(0, up_send, up_recv)
     forward_on(1, k_ref, kbuf, 1)
 
     collect(0, up_send, up_recv)
@@ -498,6 +497,10 @@
     inverse = lax.rsqrt(mean)
     factor = jnp.broadcast_to(total[:, HD // 2 : HD // 2 + 1], (BLK, HD)) / (features * mean)
     halves = [((scaled[h] - raws[h] * factor) * inverse).astype(BF16) for h in range(heads)]
+    for h in range(heads):
+        back = tn(qscaled[h], halves[h])
+        back_send[h] = back.astype(BF16)
+    spread(2, back_send, back_recv)
     mix_grads = []
     deltas = []
     gs = []
@@ -522,11 +525,6 @@
     side[...] = block.T[0 : 2 * heads, :]
     sidebuf[0] = side[...]
     send_small(6, side, sidebuf, -1)
-    for h in range(heads):
-        back = tn(qscaled[h], halves[h])
-        back_send[h] = back.astype(BF16)
-    spread(2, back_send, back_recv)
-
     leaves[5].start()
     for h in range(heads):
         lout_ref[:, cols[h]] = (raws[h] * inverse * gain_ref[:, cols[h]]).astype(BF16)
@@ -545,9 +543,9 @@
     starts, state, product = scan_plane(terms, factors, range(GROUP - 1, -1, -1))
     total_send[1] = with_tail(state, product)
     send_totals(1, -1)
+    forward_on(5, gbuf.at[0], gbuf, -1)
     key_local = [tn(mix_grads[h], outs[h]) for h in range(heads)]
     value_local = [tn(mixing[h], halves[h]) for h in range(heads)]
-    forward_on(5, gbuf.at[0], gbuf, -1)
     wait_totals(1, -1)
     state = incoming(1, planes - 1 - plane)
     for p in range(GROUP):

time: 56.9 us -> 50 us (0.88)
  Pallas kernels: 55.5 us -> 48.6 us
    pallas_call x1, Pallas kernels: 53.4 us -> 46.5 us  [body(): pl.pallas_call(functools.partial(kernel, n, groups), out_shape=[jax.Shape...]
where the time goes in v6:
time: 50 us; the launch traced here: 49.9 us
  Pallas kernels  48.6 us (97%)
  between operations  1.29 us (3%)
    pallas_call x1, Pallas kernels, body(): pl.pallas_call(functools.partial(kernel, n, groups), out_shape=[jax.Shape...  46.5 us
    pallas_call x1, Pallas kernels, body(): return tuple(store(*results))  2.09 us

profile of v6, /device:TPU:0, one launch (start us, length us, event | category | flops | bytes accessed | tf_op | source)
XLA Modules:
  0.0 49.9 jit_solution(17016381880034940151)
XLA Ops:
  1.3 46.5 %shard_map.161 = (bf16[128,512]{1,0:T(8,128)(2,1)}, bf16[128,512]{1,0:T(8,128)(2,1)}, bf16[128,512]{1,0:T(8,128)(2,1)}, bf16[128,512]{1,0:T(8,128)(2,1)}, bf16[1...) custom-call(bf16[128,512]{1,0:T(8,128)(2,1)} %q_hbm.1, ...), custom_call_target="tpu_custom_call" | custom-call | tf_op jit(solution)/shard_map/pallas_call | solution.py:640
  47.8 2.1 %shard_map.162 = (bf16[128,512]{1,0:T(8,128)(2,1)}, bf16[128,512]{1,0:T(8,128)(2,1)}, bf16[128,512]{1,0:T(8,128)(2,1)}, bf16[128,512]{1,0:T(8,128)(2,1)}, bf16[1...) custom-call(bf16[128,512]{1,0:T(8,128)(2,1)} %get-tuple-element.16.refs_0_, ...), custom_call_target="tpu_custom_call" | custom-call | tf_op jit(solution)/shard_map/pallas_call | solution.py:719

commit v7 on v6

--- a/solution.py
+++ b/solution.py
@@ -497,10 +497,6 @@
     inverse = lax.rsqrt(mean)
     factor = jnp.broadcast_to(total[:, HD // 2 : HD // 2 + 1], (BLK, HD)) / (features * mean)
     halves = [((scaled[h] - raws[h] * factor) * inverse).astype(BF16) for h in range(heads)]
-    for h in range(heads):
-        back = tn(qscaled[h], halves[h])
-        back_send[h] = back.astype(BF16)
-    spread(2, back_send, back_recv)
     mix_grads = []
     deltas = []
     gs = []
@@ -513,6 +509,10 @@
         gbuf[0, :, cols[h]] = g
         gs.append(g)
     send_across(5, gbuf.at[0], -1)
+    for h in range(heads):
+        back = tn(qscaled[h], halves[h])
+        back_send[h] = back.astype(BF16)
+    spread(2, back_send, back_recv)
     send_direct(5, gbuf.at[0], gbuf, -1)
     for h in range(heads):
         g = gs[h]
@@ -529,21 +529,25 @@
     for h in range(heads):
         lout_ref[:, cols[h]] = (raws[h] * inverse * gain_ref[:, cols[h]]).astype(BF16)
     leaves[4].start()
-    for h in range(heads):
+    def query_gradient(h):
         chance = jnp.exp(score[h] - logsum[h])
         cg = nt(gbuf[0, :, cols[h]], vbuf[:, :, cols[h]].reshape(-1, HD))
         sg = (chance * (cg - deltas[h])).astype(BF16)
         keys = kbuf[:, :, cols[h]].reshape(-1, HD)
         dq_ref[:, cols[h]] = (nn(sg, keys) * scaling).astype(BF16)
-    leaves[1].start()
-
+
+    for h in range(heads // 2):
+        query_gradient(h)
+    forward_on(5, gbuf.at[0], gbuf, -1)
     collect(2, back_send, back_recv)
     terms = [back_recv[p].astype(F32) for p in range(GROUP)]
     factors = [tail_of(up_recv[p]) for p in range(GROUP)]
     starts, state, product = scan_plane(terms, factors, range(GROUP - 1, -1, -1))
     total_send[1] = with_tail(state, product)
     send_totals(1, -1)
-    forward_on(5, gbuf.at[0], gbuf, -1)
+    for h in range(heads // 2, heads):
+        query_gradient(h)
+    leaves[1].start()
     key_local = [tn(mix_grads[h], outs[h]) for h in range(heads)]
     value_local = [tn(mixing[h], halves[h]) for h in range(heads)]
     wait_totals(1, -1)

time: 50 us -> 50.3 us (level)
  no operation moved by 1% of the time
where the time goes in v7:
time: 50.3 us; the launch traced here: 50.2 us
  Pallas kernels  48.9 us (97%)
  between operations  1.29 us (3%)
    pallas_call x1, Pallas kernels, body(): pl.pallas_call(functools.partial(kernel, n, groups), out_shape=[jax.Shape...  46.8 us
    pallas_call x1, Pallas kernels, body(): return tuple(store(*results))  2.09 us

profile of v7, /device:TPU:0, one launch (start us, length us, event | category | flops | bytes accessed | tf_op | source)
XLA Modules:
  0.0 50.2 jit_solution(12130325431689776027)
XLA Ops:
  1.3 46.8 %shard_map.161 = (bf16[128,512]{1,0:T(8,128)(2,1)}, bf16[128,512]{1,0:T(8,128)(2,1)}, bf16[128,512]{1,0:T(8,128)(2,1)}, bf16[128,512]{1,0:T(8,128)(2,1)}, bf16[1...) custom-call(bf16[128,512]{1,0:T(8,128)(2,1)} %q_hbm.1, ...), custom_call_target="tpu_custom_call" | custom-call | tf_op jit(solution)/shard_map/pallas_call | solution.py:644
  48.1 2.1 %shard_map.162 = (bf16[128,512]{1,0:T(8,128)(2,1)}, bf16[128,512]{1,0:T(8,128)(2,1)}, bf16[128,512]{1,0:T(8,128)(2,1)}, bf16[128,512]{1,0:T(8,128)(2,1)}, bf16[1...) custom-call(bf16[128,512]{1,0:T(8,128)(2,1)} %get-tuple-element.16.refs_0_, ...), custom_call_target="tpu_custom_call" | custom-call | tf_op jit(solution)/shard_map/pallas_call | solution.py:723
